TPU v7x, 32 devices: a whole 2x2x4 slice. The times are simulated.
32 devices in a mesh: prompt: 8 (over y, x, core), sample: 4 (over z).
Axes of the slice: x: 2, y: 2, z: 4, core: 2. Of those that a mesh axis runs over, the one named last changes fastest.
Arguments:
- queries: bfloat16 [8, 4, 4, 8192], P('prompt', 'sample'), may hold values from -24 to 24
- new_kv: bfloat16 [8, 4, 4, 2, 1024], P('prompt', 'sample'), may hold values from -24 to 24
- suffix_kv: bfloat16 [8, 4, 256, 2, 1024], P('prompt', 'sample'), may hold values from -24 to 24
- suffix_len: int32 [8, 4], P('prompt', 'sample'), may hold values from 1 to 256, as said below
- prefix_head: bfloat16 [8, 512, 2, 1024], P('prompt', 'sample'), may hold values from -24 to 24
- prefix_tail: bfloat16 [8, 512, 2, 1024], P('prompt', 'sample'), may hold values from -24 to 24
- prefix_len: int32 [8], replicated, may hold values from 256 to 1024, as said below
Outputs:
- attended: bfloat16 [8, 4, 4, 8192], P('prompt', 'sample')
Inputs may be any that keep to these rules, and one draw needn't show every extreme that they name: `suffix_len`: some sample has all 256 slots live and some only one. `prefix_len`: some prompt has all 1024 positions live and some only 256.
All inputs are finite; a program needn't handle non-finite values.
Results may differ from a plain program's by a relative error of at most 0.001.
Values may be sent and summed in bfloat16 or wider, within the bound.
A program may use at most 64 MiB of HBM per device.

v0:
```python
import jax
import jax.numpy as jnp
from jax import lax
from jax.sharding import PartitionSpec as P

QH = 64
KVH = 8
HEAD_SIZE = 128


NEG = -1e30


def from_behind(value, axis, steps):
    count = lax.axis_size(axis)
    pairs = [(source, (source + steps) % count) for source in range(count)]
    return lax.ppermute(value, axis, pairs)


def apply_weights(logit_scores, valid_mask, value_matrix, form):
    masked = jnp.where(valid_mask, logit_scores, NEG)
    maxima = jnp.max(masked, axis=-1)
    weights = jnp.where(valid_mask, jnp.exp(masked - maxima[..., None]), 0.0)
    totals = jnp.sum(weights, axis=-1)
    numerator = jnp.einsum(form, weights, value_matrix, precision=lax.Precision.HIGHEST)
    leading = numerator.shape[:2]
    return (
        numerator.reshape(leading + (QH, HEAD_SIZE)),
        maxima.reshape(leading + (QH,)),
        totals.reshape(leading + (QH,)),
    )


def prefix_terms(query_rows, pairs, start, length):
    sample_count, step_count = (query_rows.shape[0], query_rows.shape[1])
    block_len = pairs.shape[0]
    grouped_queries = query_rows.reshape(sample_count, step_count, KVH, QH // KVH, HEAD_SIZE)
    key_matrix = pairs[:, 0].reshape(block_len, KVH, HEAD_SIZE)
    value_matrix = pairs[:, 1].reshape(block_len, KVH, HEAD_SIZE).astype(jnp.float32)
    logit_scores = jnp.einsum(
        "rhlxf,vlf->rhlxv", grouped_queries, key_matrix, preferred_element_type=jnp.float32
    ) * HEAD_SIZE ** (-0.5)
    valid_mask = start + jnp.arange(block_len, dtype=jnp.int32) < length
    return apply_weights(logit_scores, valid_mask, value_matrix, "urpyj,jpi->urpyi")


def suffix_terms(query_rows, cache, fresh, length):
    sample_count, step_count = (query_rows.shape[0], query_rows.shape[1])
    slots = cache.shape[1]
    joined = jnp.concatenate([cache, fresh], axis=1)
    total_len = joined.shape[1]
    grouped_queries = query_rows.reshape(sample_count, step_count, KVH, QH // KVH, HEAD_SIZE)
    key_matrix = joined[:, :, 0].reshape(sample_count, total_len, KVH, HEAD_SIZE)
    value_matrix = (
        joined[:, :, 1].reshape(sample_count, total_len, KVH, HEAD_SIZE).astype(jnp.float32)
    )
    logit_scores = jnp.einsum(
        "stkgd,slkd->stkgl", grouped_queries, key_matrix, preferred_element_type=jnp.float32
    ) * HEAD_SIZE ** (-0.5)
    cache_live = jnp.arange(slots, dtype=jnp.int32)[None, :] < length[:, None]
    steps_live = (
        jnp.arange(step_count, dtype=jnp.int32)[None, :]
        <= jnp.arange(step_count, dtype=jnp.int32)[:, None]
    )
    valid_mask = jnp.concatenate(
        [
            jnp.broadcast_to(cache_live[:, None, :], (sample_count, step_count, slots)),
            steps_live[None],
        ],
        axis=2,
    )
    return apply_weights(
        logit_scores, valid_mask[:, :, None, None, :], value_matrix, "stkgl,slkd->stkgd"
    )


def join(former, latter):
    maxima = jnp.maximum(former[1], latter[1])
    scale_a = jnp.exp(former[1] - maxima)
    scale_b = jnp.exp(latter[1] - maxima)
    return (
        former[0] * scale_a[..., None] + latter[0] * scale_b[..., None],
        maxima,
        former[2] * scale_a + latter[2] * scale_b,
    )


def settle(stacked):
    maxima = jnp.max(stacked[1], axis=0)
    factors = jnp.exp(stacked[1] - maxima[None])
    return (
        jnp.sum(stacked[0] * factors[..., None], axis=0),
        maxima,
        jnp.sum(stacked[2] * factors, axis=0),
    )


def spread(partial_sums):
    return (
        lax.all_to_all(partial_sums[0][None], "sample", split_axis=1, concat_axis=0, tiled=True),
        lax.all_to_all(partial_sums[1][None], "sample", split_axis=1, concat_axis=0, tiled=True),
        lax.all_to_all(partial_sums[2][None], "sample", split_axis=1, concat_axis=0, tiled=True),
    )


def per_device(queries, new_kv, suffix_kv, suffix_len, prefix_head, prefix_tail, prefix_len):
    sample_count = lax.axis_size("sample")
    prompt_row = lax.axis_index("prompt")
    sample_slot = lax.axis_index("sample")
    block_len = prefix_head.shape[1]
    half_len = block_len * sample_count
    own_length = prefix_len[prompt_row]
    local_rows = queries[0]
    every_rows = lax.all_gather(queries, "sample", axis=1, tiled=True)[0]
    near_part = suffix_terms(local_rows, suffix_kv[0], new_kv[0], suffix_len[0])
    moved = from_behind(prefix_tail, "prompt", -1)
    own_part = prefix_terms(every_rows, prefix_head[0], sample_slot * block_len, own_length)
    tail_part = prefix_terms(every_rows, moved[0], half_len + sample_slot * block_len, own_length)
    result = join(settle(spread(join(own_part, tail_part))), near_part)
    attended = (result[0] / result[2][..., None]).astype(jnp.bfloat16)
    return attended.reshape(queries.shape)


def solution(mesh):
    in_specs = (
        P("prompt", "sample", None, None),
        P("prompt", "sample", None, None, None),
        P("prompt", "sample", None, None, None),
        P("prompt", "sample"),
        P("prompt", "sample", None, None),
        P("prompt", "sample", None, None),
        P(),
    )
    out_specs = P("prompt", "sample", None, None)
    return jax.shard_map(
        per_device, mesh=mesh, in_specs=in_specs, out_specs=out_specs, check_vma=False
    )
```

profile of v0, /device:TPU:0, one launch (start us, length us, event | category | flops | bytes accessed | tf_op | source)
XLA Modules:
  0.0 74.3 jit_solution(2184970375229859384)
XLA Ops:
  0.0 1.4 %copy.58 = bf16[1,128,2,1024]{1,3,2,0:T(8,128)(2,1)S(1)} copy(bf16[1,128,2,1024]{3,2,1,0:T(2,128)(2,1)} %param.12) | data formatting | bytes 1048576 | tf_op args[5]
  1.4 3.4 %collective-permute-start = (bf16[1,128,2,1024]{1,3,2,0:T(8,128)(2,1)S(1)}, bf16[1,128,2,1024]{1,3,2,0:T(8,128)(2,1)S(1)}, u32[]{:S(2)}, u32[]{:S(2)}) collective-permute-start(bf16[1,128,2,1024]{1,3,2,0:T(8,128)(2,1)S(1)} %copy.58), channel_id=1, source_target_pairs={{0,28},{4,0},{8,4},{12,8},{16,12},{20,16},{24,20},{28,24},{1,29},{... | collective-permute-start | bytes 1572872 | tf_op jit(solution)/shard_map/ppermute | solution.py:17
  5.5 0.6 dynamic_slice.3
  6.1 0.7 add_compare_fusion.1
  6.8 14.1 %all_gather.3 = bf16[1,4,4,8192]{3,2,0,1:T(4,128)(2,1)S(1)} all-gather(bf16[1,1,4,8192]{3,2,0,1:T(4,128)(2,1)S(1)} %bitcast.151), channel_id=1, replica_groups=mesh['prompt'=8,'sample'=4] {'sample'}, dimensions={1}, use_global_device_ids=true | all-gather | bytes 327680 | tf_op jit(solution)/shard_map/all_gather | solution.py:114
  21.2 0.5 copy.51
  21.8 0.7 fusion.42
  22.5 10.4 %fusion.6 = (bf16[260,1024]{1,0:T(8,128)(2,1)S(1)}, bf16[260,1024]{1,0:T(8,128)(2,1)S(1)}) fusion(bf16[1,4,2,1024]{3,2,1,0:T(2,128)(2,1)S(1)} %bitcast.159, bf16[1,256,2,1024]{3,2,1,0:T(2,128)(2,1)S(1)} %bitcast.141), kind=kLoop, calls=%fused_computation.14 | loop fusion | flops 2129920 | bytes 2129920 | tf_op jit(solution)/shard_map/slice | solution.py:55
  34.6 0.7 add_compare_fusion
  35.9 1.6 %convolution_bitcast_fusion.1 = f32[4,4,8,8,128]{4,3,1,0,2:T(8,128)S(1)} fusion(bf16[128,8,128,1,1]{0,2,4,3,1:T(8,128)(2,1)} %bitcast.147, f32[4,4,8,8,128]{4,3,1,0,2:T(8,128)S(1)} %get-tuple-element.23, f32[4,4,8,8]{3,1,0,2:T(4,128)S(1)} %get-tuple-element.22, pred[128]{0:T(512)(128)(4,1)S(1)} %add_compare_fusion.1), kind=kOutput, calls=%fused_computation.1 | convolution fusion | flops 201588736 | bytes 1314944 | tf_op jit(solution)/shard_map/urpyj,jpi->urpyi/dot_general | solution.py:25
  38.6 0.7 convolution_bitcast_fusion
  39.4 0.7 reshape.436
  40.1 4.6 %all-to-all-start.1 = ((f32[4,1,256]{2,1,0:T(1,128)}), f32[4,1,256]{2,1,0:T(1,128)S(1)}, u32[]{:S(2)}, u32[]{:S(2)}) async-start(f32[4,1,256]{2,1,0:T(1,128)} %reshape.436), calls=%async_computation.1 | async-start | bytes 8192 | tf_op jit(solution)/shard_map/all_to_all | solution.py:101
  44.8 0.7 reshape.438
  45.5 4.9 %all-to-all-done.1 = f32[4,1,256]{2,1,0:T(1,128)S(1)} async-done(((f32[4,1,256]{2,1,0:T(1,128)}), f32[4,1,256]{2,1,0:T(1,128)S(1)}, u32[]{:S(2)}, u32[]{:S(2)}) %all-to-all-start.1) | async-done | bytes 4128 | tf_op jit(solution)/shard_map/all_to_all | solution.py:101
  50.3 3.2 %all-to-all-start.2 = ((f32[4,1,256]{2,1,0:T(1,128)}), f32[4,1,256]{2,1,0:T(1,128)S(1)}, u32[]{:S(2)}, u32[]{:S(2)}) async-start(f32[4,1,256]{2,1,0:T(1,128)} %reshape.438), calls=%async_computation.2 | async-start | bytes 8192 | tf_op jit(solution)/shard_map/all_to_all | solution.py:102
  53.6 1.1 %fusion.11 = f32[1,4,4,64,128]{4,3,2,0,1:T(8,128)} fusion(f32[4,4,8,8,128]{4,3,1,0,2:T(8,128)S(1)} %convolution_bitcast_fusion, f32[4,4,8,8,128]{4,3,1,0,2:T(8,128)S(1)} %convolution_bitcast_fusion.1, f32[4,4,64]{2,1,0:T(4,128)S(1)} %bitcast.154, f32[4,4,64]{2,1,0:T(4,128)S(1)} %bitcast.153), kind=kLoop, calls=%fused_computation.23 | loop fusion | flops 393216 | bytes 1581056 | tf_op jit(solution)/shard_map/add | solution.py:82
  54.7 4.4 %all-to-all-done.2 = f32[4,1,256]{2,1,0:T(1,128)S(1)} async-done(((f32[4,1,256]{2,1,0:T(1,128)}), f32[4,1,256]{2,1,0:T(1,128)S(1)}, u32[]{:S(2)}, u32[]{:S(2)}) %all-to-all-start.2) | async-done | bytes 4128 | tf_op jit(solution)/shard_map/all_to_all | solution.py:102
  59.1 3.5 %all-to-all-start = ((f32[1,4,4,64,128]{4,3,2,0,1:T(8,128)}), f32[1,4,4,64,128]{4,3,2,0,1:T(8,128)S(1)}, u32[]{:S(2)}, u32[]{:S(2)}) async-start(f32[1,4,4,64,128]{4,3,2,0,1:T(8,128)} %fusion.11), calls=%async_computation | async-start | bytes 1048576 | tf_op jit(solution)/shard_map/all_to_all | solution.py:100
  62.6 0.5 convolution_bitcast_fusion.2
  63.7 0.7 reduce.10
  64.4 0.7 reduce.11
  65.3 7.6 %all-to-all-done = f32[1,4,4,64,128]{4,3,2,0,1:T(8,128)S(1)} async-done(((f32[1,4,4,64,128]{4,3,2,0,1:T(8,128)}), f32[1,4,4,64,128]{4,3,2,0,1:T(8,128)S(1)}, u32[]{:S(2)}, u32[]{:S(2)}) %all-to-all-start) | async-done | bytes 524320 | tf_op jit(solution)/shard_map/all_to_all | solution.py:100
  73.6 0.7 copy.77
  (56 shorter events, 5.3 us)
Async XLA Ops:
  0.0 5.5 %copy-start.4 = (s32[8]{0:T(128)S(1)}, s32[8]{0:T(128)}, u32[]{:S(2)}) copy-start(s32[8]{0:T(128)} %param.13) | copy-start | bytes 100
  0.0 6.8 %copy-start.2 = (bf16[1,1,4,8192]{3,2,1,0:T(4,128)(2,1)S(1)}, bf16[1,1,4,8192]{3,2,1,0:T(4,128)(2,1)}, u32[]{:S(2)}) copy-start(bf16[1,1,4,8192]{3,2,1,0:T(4,128)(2,1)} %param.7) | copy-start | bytes 196612
  0.0 21.2 %copy-start.1 = (bf16[1,128,2,1024]{3,2,1,0:T(2,128)(2,1)S(1)}, bf16[1,128,2,1024]{3,2,1,0:T(2,128)(2,1)}, u32[]{:S(2)}) copy-start(bf16[1,128,2,1024]{3,2,1,0:T(2,128)(2,1)} %param.11) | copy-start | bytes 1572868
  1.4 36.1 %collective-permute-start = (bf16[1,128,2,1024]{1,3,2,0:T(8,128)(2,1)S(1)}, bf16[1,128,2,1024]{1,3,2,0:T(8,128)(2,1)S(1)}, u32[]{:S(2)}, u32[]{:S(2)}) collective-permute-start(bf16[1,128,2,1024]{1,3,2,0:T(8,128)(2,1)S(1)} %copy.58), channel_id=1, source_target_pairs={{0,28},{4,0},{8,4},{12,8},{16,12},{20,16},{24,20},{28,24},{1,29},{... | collective-permute-start | bytes 1572872 | tf_op jit(solution)/shard_map/ppermute | solution.py:17
  21.2 1.3 %copy-start = (bf16[1,1,256,2,1024]{4,3,2,1,0:T(2,128)(2,1)S(1)}, bf16[1,1,256,2,1024]{4,3,2,1,0:T(2,128)(2,1)}, u32[]{:S(2)}) copy-start(bf16[1,1,256,2,1024]{4,3,2,1,0:T(2,128)(2,1)} %param.9) | copy-start | bytes 3145732
  21.2 1.3 %copy-start.3 = (bf16[1,1,4,2,1024]{4,3,2,1,0:T(2,128)(2,1)S(1)}, bf16[1,1,4,2,1024]{4,3,2,1,0:T(2,128)(2,1)}, u32[]{:S(2)}) copy-start(bf16[1,1,4,2,1024]{4,3,2,1,0:T(2,128)(2,1)} %param.8) | copy-start | bytes 49156
  40.1 10.2 %all-to-all-start.1 = ((f32[4,1,256]{2,1,0:T(1,128)}), f32[4,1,256]{2,1,0:T(1,128)S(1)}, u32[]{:S(2)}, u32[]{:S(2)}) async-start(f32[4,1,256]{2,1,0:T(1,128)} %reshape.436), calls=%async_computation.1 | async-start | bytes 8192 | tf_op jit(solution)/shard_map/all_to_all | solution.py:101
  50.3 8.8 %all-to-all-start.2 = ((f32[4,1,256]{2,1,0:T(1,128)}), f32[4,1,256]{2,1,0:T(1,128)S(1)}, u32[]{:S(2)}, u32[]{:S(2)}) async-start(f32[4,1,256]{2,1,0:T(1,128)} %reshape.438), calls=%async_computation.2 | async-start | bytes 8192 | tf_op jit(solution)/shard_map/all_to_all | solution.py:102
  59.1 13.7 %all-to-all-start = ((f32[1,4,4,64,128]{4,3,2,0,1:T(8,128)}), f32[1,4,4,64,128]{4,3,2,0,1:T(8,128)S(1)}, u32[]{:S(2)}, u32[]{:S(2)}) async-start(f32[1,4,4,64,128]{4,3,2,0,1:T(8,128)} %fusion.11), calls=%async_computation | async-start | bytes 1048576 | tf_op jit(solution)/shard_map/all_to_all | solution.py:100
where the time goes:
time: 74.7 us; the launch traced here: 74.3 us
  waiting for transfers between devices  16.9 us (23%)
  other arithmetic  15.9 us (21%)
  starting transfers between devices  14.7 us (20%)
  blocking collectives  14.1 us (19%)
  local copies, waits for them, and re-layouts  7.64 us (10%)
  matrix products  4.01 us (5%)
  between operations  0.97 us (1%)
    all_gather x1, blocking collectives, per_device(): every_rows = lax.all_gather(queries, 'sample', axis=1, tiled=True)[0]  14.1 us
    slice x1, other arithmetic, suffix_terms(): joined[:, :, 1].reshape(sample_count, total_len, KVH, HEAD_SIZE)  10.4 us
    all_to_all x1, waiting for transfers between devices, spread(): lax.all_to_all(partial_sums[0][None], 'sample', split_axis=1, concat_axis...  7.61 us
    all_to_all x1, waiting for transfers between devices, spread(): lax.all_to_all(partial_sums[1][None], 'sample', split_axis=1, concat_axis...  4.89 us
    all_to_all x1, starting transfers between devices, spread(): lax.all_to_all(partial_sums[1][None], 'sample', split_axis=1, concat_axis...  4.64 us
    all_to_all x1, waiting for transfers between devices, spread(): lax.all_to_all(partial_sums[2][None], 'sample', split_axis=1, concat_axis...  4.41 us
    unnamed x18, local copies, waits for them, and re-layouts  3.71 us
    all_to_all x1, starting transfers between devices, spread(): lax.all_to_all(partial_sums[0][None], 'sample', split_axis=1, concat_axis...  3.47 us
  transfers between devices with their start and end apart: 4, of which 3 were waited for; matrix products, arithmetic and copies ran while one was open for 30% of the time, Pallas kernels for 0%

commit v1 on v0

v1 whole, which is shorter than its diff:
```python
import functools

import jax
import jax.numpy as jnp
from jax import lax
from jax.experimental import pallas as pl
from jax.experimental.pallas import tpu as pltpu
from jax.sharding import PartitionSpec as P

KVH = 8
HEAD_SIZE = 128
NEG = -1e30
FLOOR = -1e29
PAIR = 2
MESH = pl.DeviceIdType.MESH
F32 = jnp.float32
BF16 = jnp.bfloat16


def softmax_sums(rows, pairs, bias):
    scores = lax.dot_general(rows, pairs, (((1,), (1,)), ((), ())), preferred_element_type=F32)
    masked = scores * HEAD_SIZE ** (-0.5) + bias
    maxima = jnp.maximum(jnp.max(masked, axis=1, keepdims=True), FLOOR)
    weights = jnp.exp(masked - maxima)
    totals = jnp.sum(weights, axis=1, keepdims=True)
    weights = pltpu.roll(weights, 1, 1)
    high = weights.astype(BF16)
    low = (weights - high.astype(F32)).astype(BF16)
    numerator = jnp.dot(high, pairs, preferred_element_type=F32) + jnp.dot(
        low, pairs, preferred_element_type=F32
    )
    return numerator, maxima, totals


def put_stats(stats, lane, head, maxima, totals):
    return jnp.where(lane == head, maxima, jnp.where(lane == KVH + head, totals, stats))


def kernel(
    samples, prompts,
    plen_ref, slen_ref, q_ref, new_ref, suf_ref, head_ref, tail_ref, o_ref,
    qall, keys, stage, sufs, nsend, nrecv, ssend, srecv, near,
    lsem, qs_sem, qr_sem, ts_sem, tr_sem, ns_sem, nr_sem, ss_sem, sr_sem,
):
    row, me = lax.axis_index("prompt"), lax.axis_index("sample")
    steps = q_ref.shape[0]
    group = q_ref.shape[1] // (KVH * HEAD_SIZE)
    rows = steps * group
    block = head_ref.shape[0]
    slots = suf_ref.shape[0]
    chunks = KVH // PAIR
    above = lax.rem(row + prompts - 1, prompts)
    below = lax.rem(row + 1, prompts)

    def lanes(g):
        return pl.ds(g * HEAD_SIZE, HEAD_SIZE)

    def local(kind, g):
        source = (tail_ref, suf_ref, new_ref, head_ref)[kind]
        target = (
            lambda: stage.at[g],
            lambda: sufs.at[g, pl.ds(0, slots)],
            lambda: sufs.at[g, pl.ds(slots, steps)],
            lambda: keys.at[g, pl.ds(0, block)],
        )[kind]
        return pltpu.make_async_copy(source.at[:, :, lanes(g)], target(), lsem.at[kind, g])

    for g in range(KVH):
        local(0, g).start()

    barrier = pltpu.get_barrier_semaphore()
    for d in range(1, samples):
        pl.semaphore_signal(
            barrier, inc=1, device_id=(row, lax.rem(me + d, samples)), device_id_type=MESH
        )
    pl.semaphore_signal(barrier, inc=1, device_id=(above, me), device_id_type=MESH)
    pl.semaphore_signal(barrier, inc=1, device_id=(below, me), device_id_type=MESH)

    spare = sufs.shape[1] - slots
    for g in range(KVH):
        sufs[g, pl.ds(slots, spare)] = jnp.zeros((spare, 2, HEAD_SIZE), BF16)
    for g in range(KVH):
        for kind in range(1, 4):
            local(kind, g).start()

    wide = q_ref[...].astype(F32)
    for g in range(KVH):
        parts = [
            wide[:, (g * group + x) * HEAD_SIZE : (g * group + x + 1) * HEAD_SIZE]
            for x in range(group)
        ]
        qall[0, g] = jnp.concatenate(parts, axis=0).astype(BF16)

    pl.semaphore_wait(barrier, samples + 1)

    def heads(c):
        return pl.ds(c * PAIR, PAIR)

    def q_copy(d, c):
        return pltpu.make_async_remote_copy(
            src_ref=qall.at[0, heads(c)], dst_ref=qall.at[d, heads(c)],
            send_sem=qs_sem.at[d, c], recv_sem=qr_sem.at[d, c],
            device_id=(row, lax.rem(me + d, samples)), device_id_type=MESH,
        )

    def t_copy(c):
        return pltpu.make_async_remote_copy(
            src_ref=stage.at[heads(c)], dst_ref=keys.at[heads(c), pl.ds(block, block)],
            send_sem=ts_sem.at[c], recv_sem=tr_sem.at[c],
            device_id=(above, me), device_id_type=MESH,
        )

    def n_copy(d, c):
        return pltpu.make_async_remote_copy(
            src_ref=nsend.at[d, heads(c)], dst_ref=nrecv.at[d, heads(c)],
            send_sem=ns_sem.at[d, c], recv_sem=nr_sem.at[d, c],
            device_id=(row, lax.rem(me + samples - d, samples)), device_id_type=MESH,
        )

    def s_copy(d):
        return pltpu.make_async_remote_copy(
            src_ref=ssend.at[d], dst_ref=srecv.at[d],
            send_sem=ss_sem.at[d], recv_sem=sr_sem.at[d],
            device_id=(row, lax.rem(me + samples - d, samples)), device_id_type=MESH,
        )

    for c in range(chunks):
        for d in range(1, samples):
            q_copy(d, c).start()
        for g in range(c * PAIR, (c + 1) * PAIR):
            local(0, g).wait()
        t_copy(c).start()

    shape = (rows, 2 * sufs.shape[1])
    column = lax.broadcasted_iota(jnp.int32, shape, 1)
    step = lax.rem(lax.broadcasted_iota(jnp.int32, shape, 0), steps)
    place = column // 2
    live = (place < slen_ref[0, 0]) | ((place >= slots) & (place - slots <= step))
    near_bias = jnp.where(live & (lax.rem(column, 2) == 0), 0.0, NEG).astype(F32)
    lane = lax.broadcasted_iota(jnp.int32, (rows, HEAD_SIZE), 1)

    def near_head(g, stats):
        for kind in range(1, 3):
            local(kind, g).wait()
        pairs = sufs.at[g].reshape(2 * sufs.shape[1], HEAD_SIZE)[...]
        numerator, maxima, totals = softmax_sums(qall[0, g], pairs, near_bias)
        near[g] = numerator
        return put_stats(stats, lane, g, maxima, totals)

    near_stats = lax.fori_loop(0, KVH, near_head, jnp.full((rows, HEAD_SIZE), 0.0, F32))

    column = lax.broadcasted_iota(jnp.int32, (1, 4 * block), 1)
    place = column // 2
    place = jnp.where(place < block, place + me * block, place + (samples + me - 1) * block)
    far_bias = jnp.where((place < plen_ref[row]) & (lax.rem(column, 2) == 0), 0.0, NEG).astype(F32)
    every = samples * rows
    far_lane = lax.broadcasted_iota(jnp.int32, (every, HEAD_SIZE), 1)

    def far_chunk(c, stats):
        for d in range(1, samples):
            q_copy(d, c).wait_recv()
        t_copy(c).wait_recv()
        for i in range(PAIR):
            g = c * PAIR + i
            local(3, g).wait()
            pairs = keys.at[g].reshape(4 * block, HEAD_SIZE)[...]
            queries = qall[:, g].reshape(every, HEAD_SIZE)
            numerator, maxima, totals = softmax_sums(queries, pairs, far_bias)
            nsend[:, g] = numerator.reshape(samples, rows, HEAD_SIZE)
            stats = put_stats(stats, far_lane, g, maxima, totals)
        for d in range(1, samples):
            n_copy(d, c).start()
        return stats

    far_stats = lax.fori_loop(0, chunks, far_chunk, jnp.full((every, HEAD_SIZE), 0.0, F32))
    ssend[...] = far_stats.reshape(samples, rows, HEAD_SIZE)
    for d in range(1, samples):
        s_copy(d).start()
    for d in range(1, samples):
        s_copy(d).wait_recv()

    stats = [near_stats, ssend[0]] + [srecv[d] for d in range(1, samples)]
    peak = functools.reduce(jnp.maximum, stats)
    factors = [jnp.exp(s - peak) for s in stats]
    total = sum(pltpu.roll(s, HEAD_SIZE - KVH, 1) * f for s, f in zip(stats, factors))
    factors = [f / total for f in factors]

    for c in range(chunks):
        for d in range(1, samples):
            n_copy(d, c).wait_recv()
        for g in range(c * PAIR, (c + 1) * PAIR):
            result = near[g] * factors[0][:, g : g + 1] + nsend[0, g] * factors[1][:, g : g + 1]
            for d in range(1, samples):
                result = result + nrecv[d, g] * factors[d + 1][:, g : g + 1]
            o_ref[g] = result.astype(BF16)

    for c in range(chunks):
        t_copy(c).wait_send()
        for d in range(1, samples):
            q_copy(d, c).wait_send()
            n_copy(d, c).wait_send()
    for d in range(1, samples):
        s_copy(d).wait_send()


def per_device(queries, new_kv, suffix_kv, suffix_len, prefix_head, prefix_tail, prefix_len):
    samples = lax.axis_size("sample")
    prompts = lax.axis_size("prompt")
    steps, width = queries.shape[2:]
    group = width // (KVH * HEAD_SIZE)
    rows = steps * group
    block = prefix_head.shape[1]
    slots = suffix_kv.shape[2]
    chunks = KVH // PAIR
    near_len = slots + HEAD_SIZE // 2
    sem = pltpu.SemaphoreType.DMA
    attended = pl.pallas_call(
        functools.partial(kernel, samples, prompts),
        out_shape=jax.ShapeDtypeStruct((KVH, rows, HEAD_SIZE), BF16),
        in_specs=[pl.BlockSpec(memory_space=pltpu.SMEM)] * 2
        + [pl.BlockSpec(memory_space=pltpu.VMEM)]
        + [pl.BlockSpec(memory_space=pl.ANY)] * 4,
        out_specs=pl.BlockSpec(memory_space=pltpu.VMEM),
        scratch_shapes=[
            pltpu.VMEM((samples, KVH, rows, HEAD_SIZE), BF16),
            pltpu.VMEM((KVH, 2 * block, 2, HEAD_SIZE), BF16),
            pltpu.VMEM((KVH, block, 2, HEAD_SIZE), BF16),
            pltpu.VMEM((KVH, near_len, 2, HEAD_SIZE), BF16),
            pltpu.VMEM((samples, KVH, rows, HEAD_SIZE), F32),
            pltpu.VMEM((samples, KVH, rows, HEAD_SIZE), F32),
            pltpu.VMEM((samples, rows, HEAD_SIZE), F32),
            pltpu.VMEM((samples, rows, HEAD_SIZE), F32),
            pltpu.VMEM((KVH, rows, HEAD_SIZE), F32),
            sem((4, KVH)),
            sem((samples, chunks)), sem((samples, chunks)),
            sem((chunks,)), sem((chunks,)),
            sem((samples, chunks)), sem((samples, chunks)),
            sem((samples,)), sem((samples,)),
        ],
        compiler_params=pltpu.CompilerParams(
            collective_id=0, has_side_effects=True, vmem_limit_bytes=48 * 1024 * 1024
        ),
    )(
        prefix_len, suffix_len, queries[0, 0], new_kv[0, 0], suffix_kv[0, 0],
        prefix_head[0], prefix_tail[0],
    )
    attended = attended.reshape(KVH, group, steps, HEAD_SIZE).transpose(2, 0, 1, 3)
    return attended.reshape(queries.shape)


def solution(mesh):
    in_specs = (
        P("prompt", "sample", None, None),
        P("prompt", "sample", None, None, None),
        P("prompt", "sample", None, None, None),
        P("prompt", "sample"),
        P("prompt", "sample", None, None),
        P("prompt", "sample", None, None),
        P(),
    )
    out_specs = P("prompt", "sample", None, None)
    return jax.shard_map(
        per_device, mesh=mesh, in_specs=in_specs, out_specs=out_specs, check_vma=False
    )
```

time: 74.7 us -> 34.7 us (0.46)
  Pallas kernels: 0 us -> 27.6 us
  waiting for transfers between devices: 16.9 us -> 0 us
  other arithmetic: 15.9 us -> 0 us
  starting transfers between devices: 14.7 us -> 0 us
  blocking collectives: 14.1 us -> 0 us
  matrix products: 4.01 us -> 0 us
  local copies, waits for them, and re-layouts: 7.64 us -> 6.14 us
    pallas_call x0 -> x1, Pallas kernels: none -> 27.6 us  [per_device(): pl.pallas_call(functools.partial(kernel, samples, prompts), out_shape=jax...]
    all_to_all x3 -> x0, waiting for transfers between devices: 16.9 us -> none  [the longest x1 7.61 us: spread(): lax.all_to_all(partial_sums[0][None], 'sample', split_axis=1, concat_axis...]
    all_gather x1 -> x0, blocking collectives: 14.1 us -> none  [per_device(): every_rows = lax.all_gather(queries, 'sample', axis=1, tiled=True)[0]]
    all_to_all x3 -> x0, starting transfers between devices: 11.4 us -> none  [the longest x1 4.64 us: spread(): lax.all_to_all(partial_sums[1][None], 'sample', split_axis=1, concat_axis...]
    slice x1 -> x0, other arithmetic: 10.4 us -> none  [suffix_terms(): joined[:, :, 1].reshape(sample_count, total_len, KVH, HEAD_SIZE)]
    dot_general x6 -> x0, matrix products: 4.01 us -> none  [the longest x3 2.82 us: apply_weights(): jnp.einsum(form, weights, value_matrix, precision=lax.Precision.HIGHEST)]
    ppermute x1 -> x0, starting transfers between devices: 3.39 us -> none  [from_behind(): return lax.ppermute(value, axis, pairs)]
    unnamed x18 -> x13, local copies, waits for them, and re-layouts: 3.71 us -> 6.14 us
  transfers between devices with their start and end apart: 4 -> 0, of which waited for: 3 -> 0; matrix products, arithmetic and copies ran while one was open for 30% -> 0% of each run, Pallas kernels for 0% -> 0%
where the time goes in v1:
time: 34.7 us; the launch traced here: 34.4 us
  Pallas kernels  27.6 us (80%)
  local copies, waits for them, and re-layouts  6.14 us (18%)
  between operations  0.67 us (2%)
    pallas_call x1, Pallas kernels, per_device(): pl.pallas_call(functools.partial(kernel, samples, prompts), out_shape=jax...  27.6 us
    unnamed x13, local copies, waits for them, and re-layouts  6.14 us

profile of v1, /device:TPU:0, one launch (start us, length us, event | category | flops | bytes accessed | tf_op | source)
XLA Modules:
  0.0 34.4 jit_solution(17553425794624199158)
XLA Ops:
  0.7 0.0 copy-start.5
  0.7 0.6 %copy-done.5 = s32[8]{0:T(128)S(1)} copy-done((s32[8]{0:T(128)S(1)}, s32[8]{0:T(128)}, u32[]{:S(2)}) %copy-start.5) | copy-done | bytes 56
  1.3 0.0 copy-start
  1.3 1.2 %copy-done = bf16[1,1,256,2,1024]{4,3,2,1,0:T(2,128)(2,1)S(1)} copy-done((bf16[1,1,256,2,1024]{4,3,2,1,0:T(2,128)(2,1)S(1)}, bf16[1,1,256,2,1024]{4,3,2,1,0:T(2,128)(2,1)}, u32[]{:S(2)}) %copy-start) | copy-done | bytes 1048600
  2.5 0.0 copy-start.1
  2.5 1.0 %copy-done.1 = bf16[1,128,2,1024]{3,2,1,0:T(2,128)(2,1)S(1)} copy-done((bf16[1,128,2,1024]{3,2,1,0:T(2,128)(2,1)S(1)}, bf16[1,128,2,1024]{3,2,1,0:T(2,128)(2,1)}, u32[]{:S(2)}) %copy-start.1) | copy-done | bytes 524312
  3.6 0.0 copy-start.2
  3.6 1.0 %copy-done.2 = bf16[1,128,2,1024]{3,2,1,0:T(2,128)(2,1)S(1)} copy-done((bf16[1,128,2,1024]{3,2,1,0:T(2,128)(2,1)S(1)}, bf16[1,128,2,1024]{3,2,1,0:T(2,128)(2,1)}, u32[]{:S(2)}) %copy-start.2) | copy-done | bytes 524312
  4.6 0.0 copy-start.3
  4.6 0.8 %copy-done.3 = bf16[1,1,4,8192]{3,2,1,0:T(4,128)(2,1)S(1)} copy-done((bf16[1,1,4,8192]{3,2,1,0:T(4,128)(2,1)S(1)}, bf16[1,1,4,8192]{3,2,1,0:T(4,128)(2,1)}, u32[]{:S(2)}) %copy-start.3) | copy-done | bytes 65560
  5.5 0.0 copy-start.4
  5.5 0.7 %copy-done.4 = bf16[1,1,4,2,1024]{4,3,2,1,0:T(2,128)(2,1)S(1)} copy-done((bf16[1,1,4,2,1024]{4,3,2,1,0:T(2,128)(2,1)S(1)}, bf16[1,1,4,2,1024]{4,3,2,1,0:T(2,128)(2,1)}, u32[]{:S(2)}) %copy-start.4) | copy-done | bytes 16408
  6.2 27.6 %shard_map.73 = bf16[8,32,128]{2,1,0:T(8,128)(2,1)S(1)} custom-call(s32[8]{0:T(128)S(1)} %copy-done.5, s32[1,1]{1,0:T(1,128)S(6)} %copy.10.slen_ref, bf16[4,8192]{1,0:T(4,128)(2,1)S(1)} %bitcast.14, bf16[4,2,1024]{2,1,0:T(2,128)(2,1)S(1)} %bitcast.15, bf16[256,2,1024]{2,1,0:T(2,128)(2,1)S(1)} %bitcast.10, bf16[128,2,1024]{2,1,0:T(2,128)(2,1)S(1)} %bitcast.11, ...), custom_call_target="tpu_custom_call" | custom-call | tf_op jit(solution)/shard_map/pallas_call | solution.py:217
  33.7 0.6 %copy.11 = bf16[1,1,4,8192]{3,2,1,0:T(4,128)(2,1)} copy(bf16[1,1,4,8192]{3,2,1,0:T(4,128)(2,1)S(1)} %bitcast.13) | data formatting | bytes 131072
Async XLA Ops:
  0.7 0.7 %copy-start.5 = (s32[8]{0:T(128)S(1)}, s32[8]{0:T(128)}, u32[]{:S(2)}) copy-start(s32[8]{0:T(128)} %plen_ref.1) | copy-start | bytes 100
  1.3 1.2 %copy-start = (bf16[1,1,256,2,1024]{4,3,2,1,0:T(2,128)(2,1)S(1)}, bf16[1,1,256,2,1024]{4,3,2,1,0:T(2,128)(2,1)}, u32[]{:S(2)}) copy-start(bf16[1,1,256,2,1024]{4,3,2,1,0:T(2,128)(2,1)} %param.9) | copy-start | bytes 3145732
  2.5 1.0 %copy-start.1 = (bf16[1,128,2,1024]{3,2,1,0:T(2,128)(2,1)S(1)}, bf16[1,128,2,1024]{3,2,1,0:T(2,128)(2,1)}, u32[]{:S(2)}) copy-start(bf16[1,128,2,1024]{3,2,1,0:T(2,128)(2,1)} %param.11) | copy-start | bytes 1572868
  3.6 1.0 %copy-start.2 = (bf16[1,128,2,1024]{3,2,1,0:T(2,128)(2,1)S(1)}, bf16[1,128,2,1024]{3,2,1,0:T(2,128)(2,1)}, u32[]{:S(2)}) copy-start(bf16[1,128,2,1024]{3,2,1,0:T(2,128)(2,1)} %param.12) | copy-start | bytes 1572868
  4.6 0.8 %copy-start.3 = (bf16[1,1,4,8192]{3,2,1,0:T(4,128)(2,1)S(1)}, bf16[1,1,4,8192]{3,2,1,0:T(4,128)(2,1)}, u32[]{:S(2)}) copy-start(bf16[1,1,4,8192]{3,2,1,0:T(4,128)(2,1)} %param.7) | copy-start | bytes 196612
  5.5 0.7 %copy-start.4 = (bf16[1,1,4,2,1024]{4,3,2,1,0:T(2,128)(2,1)S(1)}, bf16[1,1,4,2,1024]{4,3,2,1,0:T(2,128)(2,1)}, u32[]{:S(2)}) copy-start(bf16[1,1,4,2,1024]{4,3,2,1,0:T(2,128)(2,1)} %param.8) | copy-start | bytes 49156

commit v2 on v1

--- a/solution.py
+++ b/solution.py
@@ -38,9 +38,9 @@
 
 def kernel(
     samples, prompts,
-    plen_ref, slen_ref, q_ref, new_ref, suf_ref, head_ref, tail_ref, o_ref,
-    qall, keys, stage, sufs, nsend, nrecv, ssend, srecv, near,
-    lsem, qs_sem, qr_sem, ts_sem, tr_sem, ns_sem, nr_sem, ss_sem, sr_sem,
+    plen_hbm, slen_hbm, q_hbm, new_ref, suf_ref, head_ref, tail_ref, o_ref,
+    plen_ref, slen_ref, q_ref, qall, keys, stage, sufs, nsend, nrecv, ssend, srecv, near,
+    asem, lsem, qs_sem, qr_sem, ts_sem, tr_sem, ns_sem, nr_sem, ss_sem, sr_sem,
 ):
     row, me = lax.axis_index("prompt"), lax.axis_index("sample")
     steps = q_ref.shape[0]
@@ -65,6 +65,13 @@
         )[kind]
         return pltpu.make_async_copy(source.at[:, :, lanes(g)], target(), lsem.at[kind, g])
 
+    arrivals = [
+        pltpu.make_async_copy(q_hbm, q_ref, asem.at[0]),
+        pltpu.make_async_copy(plen_hbm, plen_ref, asem.at[1]),
+        pltpu.make_async_copy(slen_hbm, slen_ref, asem.at[2]),
+    ]
+    for copy in arrivals:
+        copy.start()
     for g in range(KVH):
         local(0, g).start()
 
@@ -83,6 +90,8 @@
         for kind in range(1, 4):
             local(kind, g).start()
 
+    for copy in arrivals:
+        copy.wait()
     wide = q_ref[...].astype(F32)
     for g in range(KVH):
         parts = [
@@ -217,11 +226,12 @@
     attended = pl.pallas_call(
         functools.partial(kernel, samples, prompts),
         out_shape=jax.ShapeDtypeStruct((KVH, rows, HEAD_SIZE), BF16),
-        in_specs=[pl.BlockSpec(memory_space=pltpu.SMEM)] * 2
-        + [pl.BlockSpec(memory_space=pltpu.VMEM)]
-        + [pl.BlockSpec(memory_space=pl.ANY)] * 4,
+        in_specs=[pl.BlockSpec(memory_space=pl.ANY)] * 7,
         out_specs=pl.BlockSpec(memory_space=pltpu.VMEM),
         scratch_shapes=[
+            pltpu.SMEM(prefix_len.shape, jnp.int32),
+            pltpu.SMEM(suffix_len.shape, jnp.int32),
+            pltpu.VMEM((steps, width), BF16),
             pltpu.VMEM((samples, KVH, rows, HEAD_SIZE), BF16),
             pltpu.VMEM((KVH, 2 * block, 2, HEAD_SIZE), BF16),
             pltpu.VMEM((KVH, block, 2, HEAD_SIZE), BF16),
@@ -231,14 +241,14 @@
             pltpu.VMEM((samples, rows, HEAD_SIZE), F32),
             pltpu.VMEM((samples, rows, HEAD_SIZE), F32),
             pltpu.VMEM((KVH, rows, HEAD_SIZE), F32),
-            sem((4, KVH)),
+            sem((3,)), sem((4, KVH)),
             sem((samples, chunks)), sem((samples, chunks)),
             sem((chunks,)), sem((chunks,)),
             sem((samples, chunks)), sem((samples, chunks)),
             sem((samples,)), sem((samples,)),
         ],
         compiler_params=pltpu.CompilerParams(
-            collective_id=0, has_side_effects=True, vmem_limit_bytes=48 * 1024 * 1024
+            collective_id=0, has_side_effects=True, vmem_limit_bytes=64 * 1024 * 1024
         ),
     )(
         prefix_len, suffix_len, queries[0, 0], new_kv[0, 0], suffix_kv[0, 0],

time: 34.7 us -> 29.7 us (0.86)
  local copies, waits for them, and re-layouts: 6.14 us -> 1.49 us
    unnamed x13 -> x1, local copies, waits for them, and re-layouts: 6.14 us -> 1.49 us
where the time goes in v2:
time: 29.7 us; the launch traced here: 29.5 us
  Pallas kernels  27.3 us (92%)
  local copies, waits for them, and re-layouts  1.49 us (5%)
  between operations  0.66 us (2%)
    pallas_call x1, Pallas kernels, per_device(): pl.pallas_call(functools.partial(kernel, samples, prompts), out_shape=jax...  27.3 us
    unnamed x1, local copies, waits for them, and re-layouts  1.49 us

profile of v2, /device:TPU:0, one launch (start us, length us, event | category | flops | bytes accessed | tf_op | source)
XLA Modules:
  0.0 29.5 jit_solution(17284521373424032799)
XLA Ops:
  0.7 27.3 %shard_map.73 = bf16[8,32,128]{2,1,0:T(8,128)(2,1)} custom-call(s32[8]{0:T(128)} %plen_hbm.1, s32[1,1]{1,0:T(1,128)S(6)} %copy.10.slen_hbm, bf16[4,8192]{1,0:T(4,128)(2,1)} %bitcast.14, bf16[4,2,1024]{2,1,0:T(2,128)(2,1)} %bitcast.15, bf16[256,2,1024]{2,1,0:T(2,128)(2,1)} %bitcast.10, bf16[128,2,1024]{2,1,0:T(2,128)(2,1)} %bitcast.11, ...), custom_call_target="tpu_custom_call" | custom-call | tf_op jit(solution)/shard_map/pallas_call | solution.py:226
  28.0 1.5 %copy.11 = bf16[1,1,4,8192]{3,2,1,0:T(4,128)(2,1)} copy(bf16[1,1,4,8192]{3,2,1,0:T(4,128)(2,1)} %bitcast.13) | data formatting | bytes 131072

commit v3 on v2

v3 whole, which is shorter than its diff:
```python
import functools

import jax
import jax.numpy as jnp
from jax import lax
from jax.experimental import pallas as pl
from jax.experimental.pallas import tpu as pltpu
from jax.sharding import PartitionSpec as P

KVH = 8
HEAD_SIZE = 128
NEG = -1e30
FLOOR = -1e29
PAIR = 2
MESH = pl.DeviceIdType.MESH
F32 = jnp.float32
BF16 = jnp.bfloat16


def softmax_sums(rows, pairs, bias):
    scores = lax.dot_general(rows, pairs, (((1,), (1,)), ((), ())), preferred_element_type=F32)
    masked = scores * HEAD_SIZE ** (-0.5) + bias
    maxima = jnp.maximum(jnp.max(masked, axis=1, keepdims=True), FLOOR)
    weights = jnp.exp(masked - maxima)
    totals = jnp.sum(weights, axis=1, keepdims=True)
    weights = pltpu.roll(weights, 1, 1)
    high = weights.astype(BF16)
    low = (weights - high.astype(F32)).astype(BF16)
    numerator = jnp.dot(high, pairs, preferred_element_type=F32) + jnp.dot(
        low, pairs, preferred_element_type=F32
    )
    return numerator, maxima, totals


def as_rows(columns):
    count = columns[0].shape[0]
    lane = lax.broadcasted_iota(jnp.int32, (count, HEAD_SIZE), 1)
    tile = jnp.zeros((count, HEAD_SIZE), F32)
    for i, column in enumerate(columns):
        tile = jnp.where(lane == i, column, tile)
    if count < HEAD_SIZE:
        tile = jnp.concatenate([tile, jnp.zeros((HEAD_SIZE - count, HEAD_SIZE), F32)], axis=0)
    return tile.T[:8]


def join_rows(tiles):
    peak = functools.reduce(jnp.maximum, tiles)
    factors = [jnp.exp(t - peak) for t in tiles]
    totals = sum(t * pltpu.roll(f, PAIR, 0) for t, f in zip(tiles, factors))
    return peak, totals, factors


def as_columns(factors):
    row = lax.broadcasted_iota(jnp.int32, factors[0].shape, 0)
    columns = []
    for start in range(0, len(factors), 8 // PAIR):
        few = factors[start : start + 8 // PAIR]
        packed = few[0]
        for k in range(1, len(few)):
            packed = jnp.where(row < k * PAIR, packed, pltpu.roll(few[k], k * PAIR, 0))
        turned = packed.T
        for k in range(len(few)):
            columns.append([turned[:, k * PAIR + i : k * PAIR + i + 1] for i in range(PAIR)])
    return columns


def kernel(
    samples, prompts,
    plen_hbm, slen_hbm, q_hbm, new_ref, suf_ref, head_ref, tail_ref, o_ref,
    plen_ref, slen_ref, q_ref, qall, keys, stage, sufs,
    near, near_rows, nbuf, sbuf, n1, s1, cbuf, tbuf, n2, s2,
    asem, lsem, qs_sem, qr_sem, ts_sem, tr_sem, p_sem, f_sem,
):
    row, me = lax.axis_index("prompt"), lax.axis_index("sample")
    steps = q_ref.shape[0]
    group = q_ref.shape[1] // (KVH * HEAD_SIZE)
    rows = steps * group
    block = head_ref.shape[0]
    slots = suf_ref.shape[0]
    chunks = KVH // PAIR
    above = lax.rem(row + prompts - 1, prompts)
    below = lax.rem(row + 1, prompts)
    half = samples // 2

    def peer(x):
        other, bit = 0, 1
        while bit < samples:
            digit = lax.rem(me // bit, 2)
            other = other + bit * (1 - digit if x & bit else digit)
            bit *= 2
        return other

    def place_of(x):
        return (x % 2) * half + x // 2

    def lanes(g):
        return pl.ds(g * HEAD_SIZE, HEAD_SIZE)

    def local(kind, g):
        source = (tail_ref, suf_ref, new_ref, head_ref)[kind]
        target = (
            lambda: stage.at[g],
            lambda: sufs.at[g, pl.ds(0, slots)],
            lambda: sufs.at[g, pl.ds(slots, steps)],
            lambda: keys.at[g, pl.ds(0, block)],
        )[kind]
        return pltpu.make_async_copy(source.at[:, :, lanes(g)], target(), lsem.at[kind, g])

    arrivals = [
        pltpu.make_async_copy(q_hbm, q_ref, asem.at[0]),
        pltpu.make_async_copy(plen_hbm, plen_ref, asem.at[1]),
        pltpu.make_async_copy(slen_hbm, slen_ref, asem.at[2]),
    ]
    for copy in arrivals:
        copy.start()
    for g in range(KVH):
        local(0, g).start()

    barrier = pltpu.get_barrier_semaphore()
    for x in range(1, samples):
        pl.semaphore_signal(barrier, inc=1, device_id=(row, peer(x)), device_id_type=MESH)
    pl.semaphore_signal(barrier, inc=1, device_id=(above, me), device_id_type=MESH)
    pl.semaphore_signal(barrier, inc=1, device_id=(below, me), device_id_type=MESH)

    spare = sufs.shape[1] - slots
    for g in range(KVH):
        sufs[g, pl.ds(slots, spare)] = jnp.zeros((spare, 2, HEAD_SIZE), BF16)
    for g in range(KVH):
        for kind in range(1, 4):
            local(kind, g).start()

    for copy in arrivals:
        copy.wait()
    wide = q_ref[...].astype(F32)
    for g in range(KVH):
        parts = [
            wide[:, (g * group + x) * HEAD_SIZE : (g * group + x + 1) * HEAD_SIZE]
            for x in range(group)
        ]
        qall[0, g] = jnp.concatenate(parts, axis=0).astype(BF16)

    pl.semaphore_wait(barrier, samples + 1)

    def heads(c):
        return pl.ds(c * PAIR, PAIR)

    def remote(source, target, send, recv, device):
        return pltpu.make_async_remote_copy(
            src_ref=source, dst_ref=target, send_sem=send, recv_sem=recv,
            device_id=device, device_id_type=MESH,
        )

    def q_copy(x, c):
        i = place_of(x)
        return remote(
            qall.at[0, heads(c)], qall.at[i, heads(c)],
            qs_sem.at[i, c], qr_sem.at[i, c], (row, peer(x)),
        )

    def t_copy(c):
        return remote(
            stage.at[heads(c)], keys.at[heads(c), pl.ds(block, block)],
            ts_sem.at[c], tr_sem.at[c], (above, me),
        )

    def pair_sums(c):
        return remote(
            nbuf.at[c, pl.ds(half, half)], n1.at[c], p_sem.at[0, c], p_sem.at[1, c], (row, peer(1))
        )

    def pair_stats(c):
        return remote(sbuf.at[c], s1.at[c], p_sem.at[2, c], p_sem.at[3, c], (row, peer(1)))

    def far_sums(e, c):
        return remote(
            cbuf.at[c, e], n2.at[c, e], f_sem.at[0, e, c], f_sem.at[1, e, c], (row, peer(2 * e))
        )

    def far_stats(e, c):
        return remote(
            tbuf.at[c], s2.at[c, e], f_sem.at[2, e, c], f_sem.at[3, e, c], (row, peer(2 * e))
        )

    for c in range(chunks):
        for x in range(1, samples):
            q_copy(x, c).start()
        for g in range(c * PAIR, (c + 1) * PAIR):
            local(0, g).wait()
        t_copy(c).start()

    shape = (rows, 2 * sufs.shape[1])
    column = lax.broadcasted_iota(jnp.int32, shape, 1)
    step = lax.rem(lax.broadcasted_iota(jnp.int32, shape, 0), steps)
    place = column // 2
    live = (place < slen_ref[0, 0]) | ((place >= slots) & (place - slots <= step))
    near_bias = jnp.where(live & (lax.rem(column, 2) == 0), 0.0, NEG).astype(F32)

    def near_chunk(c, carry):
        maxima, totals = [], []
        for i in range(PAIR):
            g = c * PAIR + i
            for kind in range(1, 3):
                local(kind, g).wait()
            pairs = sufs.at[g].reshape(2 * sufs.shape[1], HEAD_SIZE)[...]
            near[g], top, total = softmax_sums(qall[0, g], pairs, near_bias)
            maxima.append(top)
            totals.append(total)
        near_rows[c] = as_rows(maxima + totals)
        return carry

    lax.fori_loop(0, chunks, near_chunk, 0)

    column = lax.broadcasted_iota(jnp.int32, (1, 4 * block), 1)
    place = column // 2
    place = jnp.where(place < block, place + me * block, place + (samples + me - 1) * block)
    far_bias = jnp.where((place < plen_ref[row]) & (lax.rem(column, 2) == 0), 0.0, NEG).astype(F32)
    every = samples * rows

    def partial(c):
        for x in range(1, samples):
            q_copy(x, c).wait_recv()
        t_copy(c).wait_recv()
        maxima, totals = [], []
        for i in range(PAIR):
            g = c * PAIR + i
            local(3, g).wait()
            pairs = keys.at[g].reshape(4 * block, HEAD_SIZE)[...]
            queries = qall[:, g].reshape(every, HEAD_SIZE)
            numerator, top, total = softmax_sums(queries, pairs, far_bias)
            nbuf[c, :, i] = numerator.reshape(samples, rows, HEAD_SIZE)
            maxima.append(top)
            totals.append(total)
        pair_sums(c).start()
        sbuf[c] = as_rows(maxima + totals)
        pair_stats(c).start()

    def join_pair(c):
        pair_stats(c).wait_recv()
        tiles = [sbuf[c], pltpu.roll(s1[c], every // 2, 1)]
        peak, totals, factors = join_rows(tiles)
        rank = lax.broadcasted_iota(jnp.int32, peak.shape, 0)
        tbuf[c] = jnp.where(rank < PAIR, peak, totals)
        for e in range(1, half):
            far_stats(e, c).start()
        mine, other = as_columns(factors)
        pair_sums(c).wait_recv()
        for e in list(range(1, half)) + [0]:
            span = slice(e * rows, (e + 1) * rows)
            for i in range(PAIR):
                cbuf[c, e, i] = nbuf[c, e, i] * mine[i][span] + n1[c, e, i] * other[i][span]
            if e:
                far_sums(e, c).start()

    def finish(c):
        tiles = [near_rows[c], tbuf[c][:, :HEAD_SIZE]]
        for e in range(1, half):
            far_stats(e, c).wait_recv()
            tiles.append(pltpu.roll(s2[c, e], every - e * rows, 1)[:, :HEAD_SIZE])
        _, totals, factors = join_rows(tiles)
        totals = pltpu.roll(totals, 8 - PAIR, 0)
        columns = as_columns([f / totals for f in factors])
        for e in range(1, half):
            far_sums(e, c).wait_recv()
        for i in range(PAIR):
            g = c * PAIR + i
            result = near[g] * columns[0][i][:rows] + cbuf[c, 0, i] * columns[1][i][:rows]
            for e in range(1, half):
                result = result + n2[c, e, i] * columns[e + 1][i][:rows]
            flat = [result[x * steps : (x + 1) * steps] for x in range(group)]
            o_ref[:, g * group * HEAD_SIZE : (g + 1) * group * HEAD_SIZE] = jnp.concatenate(
                flat, axis=1
            ).astype(BF16)

    for c in range(chunks + 2):
        if c < chunks:
            partial(c)
        if 1 <= c <= chunks:
            join_pair(c - 1)
        if c >= 2:
            finish(c - 2)

    for c in range(chunks):
        t_copy(c).wait_send()
        pair_sums(c).wait_send()
        pair_stats(c).wait_send()
        for x in range(1, samples):
            q_copy(x, c).wait_send()
        for e in range(1, half):
            far_sums(e, c).wait_send()
            far_stats(e, c).wait_send()


def per_device(queries, new_kv, suffix_kv, suffix_len, prefix_head, prefix_tail, prefix_len):
    samples = lax.axis_size("sample")
    prompts = lax.axis_size("prompt")
    steps, width = queries.shape[2:]
    group = width // (KVH * HEAD_SIZE)
    rows = steps * group
    block = prefix_head.shape[1]
    slots = suffix_kv.shape[2]
    chunks = KVH // PAIR
    half, every = samples // 2, samples * rows
    near_len = slots + HEAD_SIZE // 2
    sem = pltpu.SemaphoreType.DMA
    attended = pl.pallas_call(
        functools.partial(kernel, samples, prompts),
        out_shape=jax.ShapeDtypeStruct((steps, width), BF16),
        in_specs=[pl.BlockSpec(memory_space=pl.ANY)] * 7,
        out_specs=pl.BlockSpec(memory_space=pltpu.VMEM),
        scratch_shapes=[
            pltpu.SMEM(prefix_len.shape, jnp.int32),
            pltpu.SMEM(suffix_len.shape, jnp.int32),
            pltpu.VMEM((steps, width), BF16),
            pltpu.VMEM((samples, KVH, rows, HEAD_SIZE), BF16),
            pltpu.VMEM((KVH, 2 * block, 2, HEAD_SIZE), BF16),
            pltpu.VMEM((KVH, block, 2, HEAD_SIZE), BF16),
            pltpu.VMEM((KVH, near_len, 2, HEAD_SIZE), BF16),
            pltpu.VMEM((KVH, rows, HEAD_SIZE), F32),
            pltpu.VMEM((chunks, 8, HEAD_SIZE), F32),
            pltpu.VMEM((chunks, samples, PAIR, rows, HEAD_SIZE), F32),
            pltpu.VMEM((chunks, 8, every), F32),
            pltpu.VMEM((chunks, half, PAIR, rows, HEAD_SIZE), F32),
            pltpu.VMEM((chunks, 8, every), F32),
            pltpu.VMEM((chunks, half, PAIR, rows, HEAD_SIZE), F32),
            pltpu.VMEM((chunks, 8, every), F32),
            pltpu.VMEM((chunks, half, PAIR, rows, HEAD_SIZE), F32),
            pltpu.VMEM((chunks, half, 8, every), F32),
            sem((3,)), sem((4, KVH)),
            sem((samples, chunks)), sem((samples, chunks)),
            sem((chunks,)), sem((chunks,)),
            sem((4, chunks)), sem((4, half, chunks)),
        ],
        compiler_params=pltpu.CompilerParams(
            collective_id=0, has_side_effects=True, vmem_limit_bytes=64 * 1024 * 1024
        ),
    )(
        prefix_len, suffix_len, queries[0, 0], new_kv[0, 0], suffix_kv[0, 0],
        prefix_head[0], prefix_tail[0],
    )
    return attended.reshape(queries.shape)


def solution(mesh):
    in_specs = (
        P("prompt", "sample", None, None),
        P("prompt", "sample", None, None, None),
        P("prompt", "sample", None, None, None),
        P("prompt", "sample"),
        P("prompt", "sample", None, None),
        P("prompt", "sample", None, None),
        P(),
    )
    out_specs = P("prompt", "sample", None, None)
    return jax.shard_map(
        per_device, mesh=mesh, in_specs=in_specs, out_specs=out_specs, check_vma=False
    )
```

time: 29.7 us -> 30.9 us (1.040)
  Pallas kernels: 27.3 us -> 28.6 us
    pallas_call x1, Pallas kernels: 27.3 us -> 28.6 us  [per_device(): pl.pallas_call(functools.partial(kernel, samples, prompts), out_shape=jax...]
where the time goes in v3:
time: 30.9 us; the launch traced here: 30.7 us
  Pallas kernels  28.6 us (93%)
  local copies, waits for them, and re-layouts  1.49 us (5%)
  between operations  0.66 us (2%)
    pallas_call x1, Pallas kernels, per_device(): pl.pallas_call(functools.partial(kernel, samples, prompts), out_shape=jax...  28.6 us
    unnamed x1, local copies, waits for them, and re-layouts  1.49 us

profile of v3, /device:TPU:0, one launch (start us, length us, event | category | flops | bytes accessed | tf_op | source)
XLA Modules:
  0.0 30.7 jit_solution(9564898962711777747)
XLA Ops:
  0.7 28.6 %shard_map.73 = bf16[4,8192]{1,0:T(4,128)(2,1)} custom-call(s32[8]{0:T(128)} %plen_hbm.1, s32[1,1]{1,0:T(1,128)S(6)} %copy.9.slen_hbm, bf16[4,8192]{1,0:T(4,128)(2,1)} %bitcast.10, bf16[4,2,1024]{2,1,0:T(2,128)(2,1)} %bitcast.11, bf16[256,2,1024]{2,1,0:T(2,128)(2,1)} %bitcast.6, bf16[128,2,1024]{2,1,0:T(2,128)(2,1)} %bitcast.7, bf16[128,2,1024]{2,1,0:T(2,128)(2,1)} %bitcast.8), custom_call_target="tpu_custom_call" | custom-call | tf_op jit(solution)/shard_map/pallas_call | solution.py:305
  29.2 1.5 %copy.10 = bf16[1,1,4,8192]{3,2,1,0:T(4,128)(2,1)} copy(bf16[1,1,4,8192]{3,2,1,0:T(4,128)(2,1)} %bitcast.9) | data formatting | bytes 131072

commit v4 on v3

--- a/solution.py
+++ b/solution.py
@@ -12,24 +12,47 @@
 NEG = -1e30
 FLOOR = -1e29
 PAIR = 2
+TILE = 16
 MESH = pl.DeviceIdType.MESH
 F32 = jnp.float32
 BF16 = jnp.bfloat16
 
 
-def softmax_sums(rows, pairs, bias):
-    scores = lax.dot_general(rows, pairs, (((1,), (1,)), ((), ())), preferred_element_type=F32)
+def softmax_sums(rows, keys, values, bias):
+    scores = lax.dot_general(rows, keys, (((1,), (1,)), ((), ())), preferred_element_type=F32)
     masked = scores * HEAD_SIZE ** (-0.5) + bias
     maxima = jnp.maximum(jnp.max(masked, axis=1, keepdims=True), FLOOR)
     weights = jnp.exp(masked - maxima)
     totals = jnp.sum(weights, axis=1, keepdims=True)
-    weights = pltpu.roll(weights, 1, 1)
     high = weights.astype(BF16)
     low = (weights - high.astype(F32)).astype(BF16)
-    numerator = jnp.dot(high, pairs, preferred_element_type=F32) + jnp.dot(
-        low, pairs, preferred_element_type=F32
+    numerator = jnp.dot(high, values, preferred_element_type=F32) + jnp.dot(
+        low, values, preferred_element_type=F32
     )
     return numerator, maxima, totals
+
+
+def permutation():
+    size = 2 * KVH * TILE
+    to = lax.broadcasted_iota(jnp.int32, (size, size), 0)
+    source = lax.rem(to, TILE) * (2 * KVH) + lax.rem(to // TILE, KVH) * 2 + to // (TILE * KVH)
+    return (lax.broadcasted_iota(jnp.int32, (size, size), 1) == source).astype(BF16)
+
+
+def take_apart(order, raw, target, first, count):
+    size = 2 * KVH * TILE
+    flat = raw.reshape(raw.shape[0] * 2, HEAD_SIZE)
+
+    def one(b, carry):
+        block = flat[pl.ds(pl.multiple_of(b * size, size), size)]
+        sorted_rows = jnp.dot(order, block, preferred_element_type=F32).astype(BF16)
+        for kind in range(2):
+            for g in range(KVH):
+                at = (kind * KVH + g) * TILE
+                target[g, kind, pl.ds(pl.multiple_of(b * TILE, TILE), TILE)] = sorted_rows[at : at + TILE]
+        return carry
+
+    lax.fori_loop(first, first + count, one, 0)
 
 
 def as_rows(columns):
@@ -67,7 +90,7 @@
 def kernel(
     samples, prompts,
     plen_hbm, slen_hbm, q_hbm, new_ref, suf_ref, head_ref, tail_ref, o_ref,
-    plen_ref, slen_ref, q_ref, qall, keys, stage, sufs,
+    plen_ref, slen_ref, q_ref, tail_raw, suf_raw, head_raw, qall, keys, stage, sufs,
     near, near_rows, nbuf, sbuf, n1, s1, cbuf, tbuf, n2, s2,
     asem, lsem, qs_sem, qr_sem, ts_sem, tr_sem, p_sem, f_sem,
 ):
@@ -75,8 +98,8 @@
     steps = q_ref.shape[0]
     group = q_ref.shape[1] // (KVH * HEAD_SIZE)
     rows = steps * group
-    block = head_ref.shape[0]
-    slots = suf_ref.shape[0]
+    block = head_ref.shape[0] // KVH
+    slots = suf_ref.shape[0] // KVH
     chunks = KVH // PAIR
     above = lax.rem(row + prompts - 1, prompts)
     below = lax.rem(row + 1, prompts)
@@ -93,19 +116,12 @@
     def place_of(x):
         return (x % 2) * half + x // 2
 
-    def lanes(g):
-        return pl.ds(g * HEAD_SIZE, HEAD_SIZE)
-
-    def local(kind, g):
-        source = (tail_ref, suf_ref, new_ref, head_ref)[kind]
-        target = (
-            lambda: stage.at[g],
-            lambda: sufs.at[g, pl.ds(0, slots)],
-            lambda: sufs.at[g, pl.ds(slots, steps)],
-            lambda: keys.at[g, pl.ds(0, block)],
-        )[kind]
-        return pltpu.make_async_copy(source.at[:, :, lanes(g)], target(), lsem.at[kind, g])
-
+    locals_ = [
+        pltpu.make_async_copy(tail_ref, tail_raw, lsem.at[0]),
+        pltpu.make_async_copy(suf_ref, suf_raw.at[pl.ds(0, slots * KVH)], lsem.at[1]),
+        pltpu.make_async_copy(new_ref, suf_raw.at[pl.ds(slots * KVH, steps * KVH)], lsem.at[2]),
+        pltpu.make_async_copy(head_ref, head_raw, lsem.at[3]),
+    ]
     arrivals = [
         pltpu.make_async_copy(q_hbm, q_ref, asem.at[0]),
         pltpu.make_async_copy(plen_hbm, plen_ref, asem.at[1]),
@@ -113,8 +129,8 @@
     ]
     for copy in arrivals:
         copy.start()
-    for g in range(KVH):
-        local(0, g).start()
+    for copy in locals_:
+        copy.start()
 
     barrier = pltpu.get_barrier_semaphore()
     for x in range(1, samples):
@@ -122,13 +138,11 @@
     pl.semaphore_signal(barrier, inc=1, device_id=(above, me), device_id_type=MESH)
     pl.semaphore_signal(barrier, inc=1, device_id=(below, me), device_id_type=MESH)
 
-    spare = sufs.shape[1] - slots
-    for g in range(KVH):
-        sufs[g, pl.ds(slots, spare)] = jnp.zeros((spare, 2, HEAD_SIZE), BF16)
-    for g in range(KVH):
-        for kind in range(1, 4):
-            local(kind, g).start()
-
+    padding = (TILE - steps) * KVH
+    suf_raw[pl.ds((slots + steps) * KVH, padding)] = jnp.zeros((padding, 2, HEAD_SIZE), BF16)
+    spare = sufs.shape[2] - slots
+    sufs[:, :, pl.ds(slots, spare)] = jnp.zeros((KVH, 2, spare, HEAD_SIZE), BF16)
+    order = permutation()
     for copy in arrivals:
         copy.wait()
     wide = q_ref[...].astype(F32)
@@ -139,6 +153,8 @@
         ]
         qall[0, g] = jnp.concatenate(parts, axis=0).astype(BF16)
 
+    locals_[0].wait()
+    take_apart(order, tail_raw, stage, 0, block // TILE)
     pl.semaphore_wait(barrier, samples + 1)
 
     def heads(c):
@@ -159,7 +175,7 @@
 
     def t_copy(c):
         return remote(
-            stage.at[heads(c)], keys.at[heads(c), pl.ds(block, block)],
+            stage.at[heads(c)], keys.at[heads(c), :, pl.ds(block, block)],
             ts_sem.at[c], tr_sem.at[c], (above, me),
         )
 
@@ -184,25 +200,22 @@
     for c in range(chunks):
         for x in range(1, samples):
             q_copy(x, c).start()
-        for g in range(c * PAIR, (c + 1) * PAIR):
-            local(0, g).wait()
         t_copy(c).start()
-
-    shape = (rows, 2 * sufs.shape[1])
-    column = lax.broadcasted_iota(jnp.int32, shape, 1)
+    for copy in locals_[1:]:
+        copy.wait()
+    take_apart(order, suf_raw, sufs, 0, slots // TILE + 1)
+
+    shape = (rows, sufs.shape[2])
+    place = lax.broadcasted_iota(jnp.int32, shape, 1)
     step = lax.rem(lax.broadcasted_iota(jnp.int32, shape, 0), steps)
-    place = column // 2
     live = (place < slen_ref[0, 0]) | ((place >= slots) & (place - slots <= step))
-    near_bias = jnp.where(live & (lax.rem(column, 2) == 0), 0.0, NEG).astype(F32)
+    near_bias = jnp.where(live, 0.0, NEG).astype(F32)
 
     def near_chunk(c, carry):
         maxima, totals = [], []
         for i in range(PAIR):
             g = c * PAIR + i
-            for kind in range(1, 3):
-                local(kind, g).wait()
-            pairs = sufs.at[g].reshape(2 * sufs.shape[1], HEAD_SIZE)[...]
-            near[g], top, total = softmax_sums(qall[0, g], pairs, near_bias)
+            near[g], top, total = softmax_sums(qall[0, g], sufs[g, 0], sufs[g, 1], near_bias)
             maxima.append(top)
             totals.append(total)
         near_rows[c] = as_rows(maxima + totals)
@@ -210,10 +223,10 @@
 
     lax.fori_loop(0, chunks, near_chunk, 0)
 
-    column = lax.broadcasted_iota(jnp.int32, (1, 4 * block), 1)
-    place = column // 2
+    take_apart(order, head_raw, keys, 0, block // TILE)
+    place = lax.broadcasted_iota(jnp.int32, (1, 2 * block), 1)
     place = jnp.where(place < block, place + me * block, place + (samples + me - 1) * block)
-    far_bias = jnp.where((place < plen_ref[row]) & (lax.rem(column, 2) == 0), 0.0, NEG).astype(F32)
+    far_bias = jnp.where(place < plen_ref[row], 0.0, NEG).astype(F32)
     every = samples * rows
 
     def partial(c):
@@ -223,10 +236,8 @@
         maxima, totals = [], []
         for i in range(PAIR):
             g = c * PAIR + i
-            local(3, g).wait()
-            pairs = keys.at[g].reshape(4 * block, HEAD_SIZE)[...]
             queries = qall[:, g].reshape(every, HEAD_SIZE)
-            numerator, top, total = softmax_sums(queries, pairs, far_bias)
+            numerator, top, total = softmax_sums(queries, keys[g, 0], keys[g, 1], far_bias)
             nbuf[c, :, i] = numerator.reshape(samples, rows, HEAD_SIZE)
             maxima.append(top)
             totals.append(total)
@@ -290,6 +301,12 @@
             far_stats(e, c).wait_send()
 
 
+def by_head(pairs):
+    count = pairs.shape[0]
+    split = pairs.reshape(count, 2, KVH, HEAD_SIZE).transpose(0, 2, 1, 3)
+    return split.reshape(count * KVH, 2, HEAD_SIZE)
+
+
 def per_device(queries, new_kv, suffix_kv, suffix_len, prefix_head, prefix_tail, prefix_len):
     samples = lax.axis_size("sample")
     prompts = lax.axis_size("prompt")
@@ -300,7 +317,6 @@
     slots = suffix_kv.shape[2]
     chunks = KVH // PAIR
     half, every = samples // 2, samples * rows
-    near_len = slots + HEAD_SIZE // 2
     sem = pltpu.SemaphoreType.DMA
     attended = pl.pallas_call(
         functools.partial(kernel, samples, prompts),
@@ -311,10 +327,13 @@
             pltpu.SMEM(prefix_len.shape, jnp.int32),
             pltpu.SMEM(suffix_len.shape, jnp.int32),
             pltpu.VMEM((steps, width), BF16),
+            pltpu.VMEM((block * KVH, 2, HEAD_SIZE), BF16),
+            pltpu.VMEM(((slots + TILE) * KVH, 2, HEAD_SIZE), BF16),
+            pltpu.VMEM((block * KVH, 2, HEAD_SIZE), BF16),
             pltpu.VMEM((samples, KVH, rows, HEAD_SIZE), BF16),
-            pltpu.VMEM((KVH, 2 * block, 2, HEAD_SIZE), BF16),
-            pltpu.VMEM((KVH, block, 2, HEAD_SIZE), BF16),
-            pltpu.VMEM((KVH, near_len, 2, HEAD_SIZE), BF16),
+            pltpu.VMEM((KVH, 2, 2 * block, HEAD_SIZE), BF16),
+            pltpu.VMEM((KVH, 2, block, HEAD_SIZE), BF16),
+            pltpu.VMEM((KVH, 2, slots + HEAD_SIZE, HEAD_SIZE), BF16),
             pltpu.VMEM((KVH, rows, HEAD_SIZE), F32),
             pltpu.VMEM((chunks, 8, HEAD_SIZE), F32),
             pltpu.VMEM((chunks, samples, PAIR, rows, HEAD_SIZE), F32),
@@ -325,7 +344,7 @@
             pltpu.VMEM((chunks, 8, every), F32),
             pltpu.VMEM((chunks, half, PAIR, rows, HEAD_SIZE), F32),
             pltpu.VMEM((chunks, half, 8, every), F32),
-            sem((3,)), sem((4, KVH)),
+            sem((3,)), sem((4,)),
             sem((samples, chunks)), sem((samples, chunks)),
             sem((chunks,)), sem((chunks,)),
             sem((4, chunks)), sem((4, half, chunks)),
@@ -334,8 +353,8 @@
             collective_id=0, has_side_effects=True, vmem_limit_bytes=64 * 1024 * 1024
         ),
     )(
-        prefix_len, suffix_len, queries[0, 0], new_kv[0, 0], suffix_kv[0, 0],
-        prefix_head[0], prefix_tail[0],
+        prefix_len, suffix_len, queries[0, 0], by_head(new_kv[0, 0]), by_head(suffix_kv[0, 0]),
+        by_head(prefix_head[0]), by_head(prefix_tail[0]),
     )
     return attended.reshape(queries.shape)
 

time: 30.9 us -> 32.7 us (1.058)
  Pallas kernels: 28.6 us -> 30.3 us
    pallas_call x1, Pallas kernels: 28.6 us -> 30.3 us  [per_device(): pl.pallas_call(functools.partial(kernel, samples, prompts), out_shape=jax...]
where the time goes in v4:
time: 32.7 us; the launch traced here: 32.5 us
  Pallas kernels  30.3 us (93%)
  local copies, waits for them, and re-layouts  1.49 us (5%)
  between operations  0.66 us (2%)
    pallas_call x1, Pallas kernels, per_device(): pl.pallas_call(functools.partial(kernel, samples, prompts), out_shape=jax...  30.3 us
    unnamed x1, local copies, waits for them, and re-layouts  1.49 us

profile of v4, /device:TPU:0, one launch (start us, length us, event | category | flops | bytes accessed | tf_op | source)
XLA Modules:
  0.0 32.5 jit_solution(5663593578700052320)
XLA Ops:
  0.7 30.3 %shard_map.73 = bf16[4,8192]{1,0:T(4,128)(2,1)} custom-call(s32[8]{0:T(128)} %plen_hbm.1, s32[1,1]{1,0:T(1,128)S(6)} %copy.13.slen_hbm, bf16[4,8192]{1,0:T(4,128)(2,1)} %bitcast.26, bf16[32,2,128]{2,1,0:T(2,128)(2,1)} %bitcast.27, bf16[2048,2,128]{2,1,0:T(2,128)(2,1)} %bitcast.22, bf16[1024,2,128]{2,1,0:T(2,128)(2,1)} %bitcast.23, bf16[1024,2,128]{2,1,0:T(2,128)(2,1)} %bitcast.24), custom_call_target="tpu_custom_call" | custom-call | tf_op jit(solution)/shard_map/pallas_call | solution.py:321
  31.0 1.5 %copy.14 = bf16[1,1,4,8192]{3,2,1,0:T(4,128)(2,1)} copy(bf16[1,1,4,8192]{3,2,1,0:T(4,128)(2,1)} %bitcast.25) | data formatting | bytes 131072

commit v5 on v2

--- a/solution.py
+++ b/solution.py
@@ -12,24 +12,29 @@
 NEG = -1e30
 FLOOR = -1e29
 PAIR = 2
+FEW = 4
 MESH = pl.DeviceIdType.MESH
 F32 = jnp.float32
 BF16 = jnp.bfloat16
 
 
-def softmax_sums(rows, pairs, bias):
-    scores = lax.dot_general(rows, pairs, (((1,), (1,)), ((), ())), preferred_element_type=F32)
-    masked = scores * HEAD_SIZE ** (-0.5) + bias
-    maxima = jnp.maximum(jnp.max(masked, axis=1, keepdims=True), FLOOR)
-    weights = jnp.exp(masked - maxima)
-    totals = jnp.sum(weights, axis=1, keepdims=True)
-    weights = pltpu.roll(weights, 1, 1)
-    high = weights.astype(BF16)
-    low = (weights - high.astype(F32)).astype(BF16)
-    numerator = jnp.dot(high, pairs, preferred_element_type=F32) + jnp.dot(
-        low, pairs, preferred_element_type=F32
-    )
-    return numerator, maxima, totals
+def softmax_sums(queries, pairs, bias):
+    contract = (((1,), (1,)), ((), ()))
+    scores = [
+        lax.dot_general(q, p, contract, preferred_element_type=F32) for q, p in zip(queries, pairs)
+    ]
+    masked = [s * HEAD_SIZE ** (-0.5) + bias for s in scores]
+    maxima = [jnp.maximum(jnp.max(m, axis=1, keepdims=True), FLOOR) for m in masked]
+    weights = [jnp.exp(m - top) for m, top in zip(masked, maxima)]
+    totals = [jnp.sum(w, axis=1, keepdims=True) for w in weights]
+    weights = [pltpu.roll(w, 1, 1) for w in weights]
+    high = [w.astype(BF16) for w in weights]
+    low = [(w - h.astype(F32)).astype(BF16) for w, h in zip(weights, high)]
+    numerators = [
+        jnp.dot(h, p, preferred_element_type=F32) + jnp.dot(l, p, preferred_element_type=F32)
+        for h, l, p in zip(high, low, pairs)
+    ]
+    return numerators, maxima, totals
 
 
 def put_stats(stats, lane, head, maxima, totals):
@@ -128,7 +133,7 @@
 
     def s_copy(d):
         return pltpu.make_async_remote_copy(
-            src_ref=ssend.at[d], dst_ref=srecv.at[d],
+            src_ref=ssend, dst_ref=srecv.at[d],
             send_sem=ss_sem.at[d], recv_sem=sr_sem.at[d],
             device_id=(row, lax.rem(me + samples - d, samples)), device_id_type=MESH,
         )
@@ -136,6 +141,7 @@
     for c in range(chunks):
         for d in range(1, samples):
             q_copy(d, c).start()
+    for c in range(chunks):
         for g in range(c * PAIR, (c + 1) * PAIR):
             local(0, g).wait()
         t_copy(c).start()
@@ -148,15 +154,21 @@
     near_bias = jnp.where(live & (lax.rem(column, 2) == 0), 0.0, NEG).astype(F32)
     lane = lax.broadcasted_iota(jnp.int32, (rows, HEAD_SIZE), 1)
 
-    def near_head(g, stats):
-        for kind in range(1, 3):
-            local(kind, g).wait()
-        pairs = sufs.at[g].reshape(2 * sufs.shape[1], HEAD_SIZE)[...]
-        numerator, maxima, totals = softmax_sums(qall[0, g], pairs, near_bias)
-        near[g] = numerator
-        return put_stats(stats, lane, g, maxima, totals)
-
-    near_stats = lax.fori_loop(0, KVH, near_head, jnp.full((rows, HEAD_SIZE), 0.0, F32))
+    def near_heads(k, stats):
+        group_heads = [k * FEW + i for i in range(FEW)]
+        for g in group_heads:
+            for kind in range(1, 3):
+                local(kind, g).wait()
+        pairs = [sufs.at[g].reshape(2 * sufs.shape[1], HEAD_SIZE)[...] for g in group_heads]
+        sums = softmax_sums([qall[0, g] for g in group_heads], pairs, near_bias)
+        for g, numerator, maxima, totals in zip(group_heads, *sums):
+            near[g] = numerator
+            stats = put_stats(stats, lane, g, maxima, totals)
+        return stats
+
+    near_stats = lax.fori_loop(0, KVH // FEW, near_heads, jnp.zeros((rows, HEAD_SIZE), F32))
+    padding = jnp.zeros((HEAD_SIZE - rows, HEAD_SIZE), F32)
+    near_stats = jnp.concatenate([near_stats, padding], axis=0).T[: 2 * KVH]
 
     column = lax.broadcasted_iota(jnp.int32, (1, 4 * block), 1)
     place = column // 2
@@ -169,12 +181,13 @@
         for d in range(1, samples):
             q_copy(d, c).wait_recv()
         t_copy(c).wait_recv()
-        for i in range(PAIR):
-            g = c * PAIR + i
+        both = [c * PAIR + i for i in range(PAIR)]
+        for g in both:
             local(3, g).wait()
-            pairs = keys.at[g].reshape(4 * block, HEAD_SIZE)[...]
-            queries = qall[:, g].reshape(every, HEAD_SIZE)
-            numerator, maxima, totals = softmax_sums(queries, pairs, far_bias)
+        pairs = [keys.at[g].reshape(4 * block, HEAD_SIZE)[...] for g in both]
+        queries = [qall[:, g].reshape(every, HEAD_SIZE) for g in both]
+        sums = softmax_sums(queries, pairs, far_bias)
+        for g, numerator, maxima, totals in zip(both, *sums):
             nsend[:, g] = numerator.reshape(samples, rows, HEAD_SIZE)
             stats = put_stats(stats, far_lane, g, maxima, totals)
         for d in range(1, samples):
@@ -182,25 +195,31 @@
         return stats
 
     far_stats = lax.fori_loop(0, chunks, far_chunk, jnp.full((every, HEAD_SIZE), 0.0, F32))
-    ssend[...] = far_stats.reshape(samples, rows, HEAD_SIZE)
+    ssend[...] = far_stats.T[: 2 * KVH]
     for d in range(1, samples):
         s_copy(d).start()
     for d in range(1, samples):
         s_copy(d).wait_recv()
 
-    stats = [near_stats, ssend[0]] + [srecv[d] for d in range(1, samples)]
-    peak = functools.reduce(jnp.maximum, stats)
-    factors = [jnp.exp(s - peak) for s in stats]
-    total = sum(pltpu.roll(s, HEAD_SIZE - KVH, 1) * f for s, f in zip(stats, factors))
+    stats = [near_stats, ssend[:, :HEAD_SIZE]]
+    for d in range(1, samples):
+        stats.append(pltpu.roll(srecv[d], every - d * rows, 1)[:, :HEAD_SIZE])
+    peak = functools.reduce(jnp.maximum, [s[:KVH] for s in stats])
+    factors = [jnp.exp(s[:KVH] - peak) for s in stats]
+    total = sum(s[KVH:] * f for s, f in zip(stats, factors))
     factors = [f / total for f in factors]
+    factors = jnp.concatenate(factors, axis=0).T[:rows]
+
+    def factor(k, g):
+        return factors[:, k * KVH + g : k * KVH + g + 1]
 
     for c in range(chunks):
         for d in range(1, samples):
             n_copy(d, c).wait_recv()
         for g in range(c * PAIR, (c + 1) * PAIR):
-            result = near[g] * factors[0][:, g : g + 1] + nsend[0, g] * factors[1][:, g : g + 1]
+            result = near[g] * factor(0, g) + nsend[0, g] * factor(1, g)
             for d in range(1, samples):
-                result = result + nrecv[d, g] * factors[d + 1][:, g : g + 1]
+                result = result + nrecv[d, g] * factor(d + 1, g)
             o_ref[g] = result.astype(BF16)
 
     for c in range(chunks):
@@ -238,8 +257,8 @@
             pltpu.VMEM((KVH, near_len, 2, HEAD_SIZE), BF16),
             pltpu.VMEM((samples, KVH, rows, HEAD_SIZE), F32),
             pltpu.VMEM((samples, KVH, rows, HEAD_SIZE), F32),
-            pltpu.VMEM((samples, rows, HEAD_SIZE), F32),
-            pltpu.VMEM((samples, rows, HEAD_SIZE), F32),
+            pltpu.VMEM((2 * KVH, samples * rows), F32),
+            pltpu.VMEM((samples, 2 * KVH, samples * rows), F32),
             pltpu.VMEM((KVH, rows, HEAD_SIZE), F32),
             sem((3,)), sem((4, KVH)),
             sem((samples, chunks)), sem((samples, chunks)),

time: 29.7 us -> 28.8 us (0.970)
  Pallas kernels: 27.3 us -> 26.5 us
    pallas_call x1, Pallas kernels: 27.3 us -> 26.5 us  [per_device(): pl.pallas_call(functools.partial(kernel, samples, prompts), out_shape=jax...]
where the time goes in v5:
time: 28.8 us; the launch traced here: 28.7 us
  Pallas kernels  26.5 us (92%)
  local copies, waits for them, and re-layouts  1.49 us (5%)
  between operations  0.66 us (2%)
    pallas_call x1, Pallas kernels, per_device(): pl.pallas_call(functools.partial(kernel, samples, prompts), out_shape=jax...  26.5 us
    unnamed x1, local copies, waits for them, and re-layouts  1.49 us

profile of v5, /device:TPU:0, one launch (start us, length us, event | category | flops | bytes accessed | tf_op | source)
XLA Modules:
  0.0 28.7 jit_solution(15168384304859960218)
XLA Ops:
  0.7 26.5 %shard_map.73 = bf16[8,32,128]{2,1,0:T(8,128)(2,1)} custom-call(s32[8]{0:T(128)} %plen_hbm.1, s32[1,1]{1,0:T(1,128)S(6)} %copy.10.slen_hbm, bf16[4,8192]{1,0:T(4,128)(2,1)} %bitcast.14, bf16[4,2,1024]{2,1,0:T(2,128)(2,1)} %bitcast.15, bf16[256,2,1024]{2,1,0:T(2,128)(2,1)} %bitcast.10, bf16[128,2,1024]{2,1,0:T(2,128)(2,1)} %bitcast.11, ...), custom_call_target="tpu_custom_call" | custom-call | tf_op jit(solution)/shard_map/pallas_call | solution.py:245
  27.2 1.5 %copy.11 = bf16[1,1,4,8192]{3,2,1,0:T(4,128)(2,1)} copy(bf16[1,1,4,8192]{3,2,1,0:T(4,128)(2,1)} %bitcast.13) | data formatting | bytes 131072

commit v6 on v5

--- a/solution.py
+++ b/solution.py
@@ -57,6 +57,14 @@
     above = lax.rem(row + prompts - 1, prompts)
     below = lax.rem(row + 1, prompts)
 
+    def peer(x):
+        other, bit = 0, 1
+        while bit < samples:
+            digit = lax.rem(me // bit, 2)
+            other = other + bit * (1 - digit if x & bit else digit)
+            bit *= 2
+        return (row, other)
+
     def lanes(g):
         return pl.ds(g * HEAD_SIZE, HEAD_SIZE)
 
@@ -82,9 +90,7 @@
 
     barrier = pltpu.get_barrier_semaphore()
     for d in range(1, samples):
-        pl.semaphore_signal(
-            barrier, inc=1, device_id=(row, lax.rem(me + d, samples)), device_id_type=MESH
-        )
+        pl.semaphore_signal(barrier, inc=1, device_id=peer(d), device_id_type=MESH)
     pl.semaphore_signal(barrier, inc=1, device_id=(above, me), device_id_type=MESH)
     pl.semaphore_signal(barrier, inc=1, device_id=(below, me), device_id_type=MESH)
 
@@ -111,10 +117,11 @@
         return pl.ds(c * PAIR, PAIR)
 
     def q_copy(d, c):
+        onward = d % 2 == 1 and d > 1
         return pltpu.make_async_remote_copy(
-            src_ref=qall.at[0, heads(c)], dst_ref=qall.at[d, heads(c)],
+            src_ref=qall.at[d - 1 if onward else 0, heads(c)], dst_ref=qall.at[d, heads(c)],
             send_sem=qs_sem.at[d, c], recv_sem=qr_sem.at[d, c],
-            device_id=(row, lax.rem(me + d, samples)), device_id_type=MESH,
+            device_id=peer(1 if onward else d), device_id_type=MESH,
         )
 
     def t_copy(c):
@@ -128,18 +135,18 @@
         return pltpu.make_async_remote_copy(
             src_ref=nsend.at[d, heads(c)], dst_ref=nrecv.at[d, heads(c)],
             send_sem=ns_sem.at[d, c], recv_sem=nr_sem.at[d, c],
-            device_id=(row, lax.rem(me + samples - d, samples)), device_id_type=MESH,
+            device_id=peer(d), device_id_type=MESH,
         )
 
     def s_copy(d):
         return pltpu.make_async_remote_copy(
             src_ref=ssend, dst_ref=srecv.at[d],
             send_sem=ss_sem.at[d], recv_sem=sr_sem.at[d],
-            device_id=(row, lax.rem(me + samples - d, samples)), device_id_type=MESH,
+            device_id=peer(d), device_id_type=MESH,
         )
 
     for c in range(chunks):
-        for d in range(1, samples):
+        for d in [1] + list(range(2, samples, 2)):
             q_copy(d, c).start()
     for c in range(chunks):
         for g in range(c * PAIR, (c + 1) * PAIR):
@@ -166,7 +173,16 @@
             stats = put_stats(stats, lane, g, maxima, totals)
         return stats
 
-    near_stats = lax.fori_loop(0, KVH // FEW, near_heads, jnp.zeros((rows, HEAD_SIZE), F32))
+    def pass_on(c):
+        for d in range(2, samples, 2):
+            q_copy(d, c).wait_recv()
+            q_copy(d + 1, c).start()
+
+    near_stats = jnp.zeros((rows, HEAD_SIZE), F32)
+    for k in range(KVH // FEW):
+        near_stats = near_heads(k, near_stats)
+        for c in range(k * FEW // PAIR, (k + 1) * FEW // PAIR):
+            pass_on(c)
     padding = jnp.zeros((HEAD_SIZE - rows, HEAD_SIZE), F32)
     near_stats = jnp.concatenate([near_stats, padding], axis=0).T[: 2 * KVH]
 
@@ -178,7 +194,7 @@
     far_lane = lax.broadcasted_iota(jnp.int32, (every, HEAD_SIZE), 1)
 
     def far_chunk(c, stats):
-        for d in range(1, samples):
+        for d in range(1, samples, 2):
             q_copy(d, c).wait_recv()
         t_copy(c).wait_recv()
         both = [c * PAIR + i for i in range(PAIR)]

time: 28.8 us -> 29.1 us (1.010)
  no operation moved by 1% of the time
where the time goes in v6:
time: 29.1 us; the launch traced here: 28.9 us
  Pallas kernels  26.7 us (92%)
  local copies, waits for them, and re-layouts  1.49 us (5%)
  between operations  0.66 us (2%)
    pallas_call x1, Pallas kernels, per_device(): pl.pallas_call(functools.partial(kernel, samples, prompts), out_shape=jax...  26.7 us
    unnamed x1, local copies, waits for them, and re-layouts  1.49 us

profile of v6, /device:TPU:0, one launch (start us, length us, event | category | flops | bytes accessed | tf_op | source)
XLA Modules:
  0.0 28.9 jit_solution(12890623239975081967)
XLA Ops:
  0.7 26.7 %shard_map.73 = bf16[8,32,128]{2,1,0:T(8,128)(2,1)} custom-call(s32[8]{0:T(128)} %plen_hbm.1, s32[1,1]{1,0:T(1,128)S(6)} %copy.10.slen_hbm, bf16[4,8192]{1,0:T(4,128)(2,1)} %bitcast.14, bf16[4,2,1024]{2,1,0:T(2,128)(2,1)} %bitcast.15, bf16[256,2,1024]{2,1,0:T(2,128)(2,1)} %bitcast.10, bf16[128,2,1024]{2,1,0:T(2,128)(2,1)} %bitcast.11, ...), custom_call_target="tpu_custom_call" | custom-call | tf_op jit(solution)/shard_map/pallas_call | solution.py:261
  27.4 1.5 %copy.11 = bf16[1,1,4,8192]{3,2,1,0:T(4,128)(2,1)} copy(bf16[1,1,4,8192]{3,2,1,0:T(4,128)(2,1)} %bitcast.13) | data formatting | bytes 131072

commit v7 on v5

--- a/solution.py
+++ b/solution.py
@@ -1,4 +1,5 @@
 import functools
+import math
 
 import jax
 import jax.numpy as jnp
@@ -10,6 +11,7 @@
 KVH = 8
 HEAD_SIZE = 128
 NEG = -1e30
+SCALE = math.log2(math.e) * HEAD_SIZE ** (-0.5)
 FLOOR = -1e29
 PAIR = 2
 FEW = 4
@@ -23,9 +25,9 @@
     scores = [
         lax.dot_general(q, p, contract, preferred_element_type=F32) for q, p in zip(queries, pairs)
     ]
-    masked = [s * HEAD_SIZE ** (-0.5) + bias for s in scores]
+    masked = [s * SCALE + bias for s in scores]
     maxima = [jnp.maximum(jnp.max(m, axis=1, keepdims=True), FLOOR) for m in masked]
-    weights = [jnp.exp(m - top) for m, top in zip(masked, maxima)]
+    weights = [jnp.exp2(m - top) for m, top in zip(masked, maxima)]
     totals = [jnp.sum(w, axis=1, keepdims=True) for w in weights]
     weights = [pltpu.roll(w, 1, 1) for w in weights]
     high = [w.astype(BF16) for w in weights]
@@ -166,9 +168,7 @@
             stats = put_stats(stats, lane, g, maxima, totals)
         return stats
 
-    near_stats = lax.fori_loop(0, KVH // FEW, near_heads, jnp.zeros((rows, HEAD_SIZE), F32))
-    padding = jnp.zeros((HEAD_SIZE - rows, HEAD_SIZE), F32)
-    near_stats = jnp.concatenate([near_stats, padding], axis=0).T[: 2 * KVH]
+    near_stats = near_heads(0, jnp.zeros((rows, HEAD_SIZE), F32))
 
     column = lax.broadcasted_iota(jnp.int32, (1, 4 * block), 1)
     place = column // 2
@@ -198,6 +198,10 @@
     ssend[...] = far_stats.T[: 2 * KVH]
     for d in range(1, samples):
         s_copy(d).start()
+    for k in range(1, KVH // FEW):
+        near_stats = near_heads(k, near_stats)
+    padding = jnp.zeros((HEAD_SIZE - rows, HEAD_SIZE), F32)
+    near_stats = jnp.concatenate([near_stats, padding], axis=0).T[: 2 * KVH]
     for d in range(1, samples):
         s_copy(d).wait_recv()
 
@@ -205,7 +209,7 @@
     for d in range(1, samples):
         stats.append(pltpu.roll(srecv[d], every - d * rows, 1)[:, :HEAD_SIZE])
     peak = functools.reduce(jnp.maximum, [s[:KVH] for s in stats])
-    factors = [jnp.exp(s[:KVH] - peak) for s in stats]
+    factors = [jnp.exp2(s[:KVH] - peak) for s in stats]
     total = sum(s[KVH:] * f for s, f in zip(stats, factors))
     factors = [f / total for f in factors]
     factors = jnp.concatenate(factors, axis=0).T[:rows]

time: 28.8 us -> 28.8 us (level)
  no operation moved by 1% of the time
where the time goes in v7:
time: 28.8 us; the launch traced here: 28.7 us
  Pallas kernels  26.5 us (92%)
  local copies, waits for them, and re-layouts  1.49 us (5%)
  between operations  0.66 us (2%)
    pallas_call x1, Pallas kernels, per_device(): pl.pallas_call(functools.partial(kernel, samples, prompts), out_shape=jax...  26.5 us
    unnamed x1, local copies, waits for them, and re-layouts  1.49 us

profile of v7, /device:TPU:0, one launch (start us, length us, event | category | flops | bytes accessed | tf_op | source)
XLA Modules:
  0.0 28.7 jit_solution(1241388794846545269)
XLA Ops:
  0.7 26.5 %shard_map.73 = bf16[8,32,128]{2,1,0:T(8,128)(2,1)} custom-call(s32[8]{0:T(128)} %plen_hbm.1, s32[1,1]{1,0:T(1,128)S(6)} %copy.10.slen_hbm, bf16[4,8192]{1,0:T(4,128)(2,1)} %bitcast.14, bf16[4,2,1024]{2,1,0:T(2,128)(2,1)} %bitcast.15, bf16[256,2,1024]{2,1,0:T(2,128)(2,1)} %bitcast.10, bf16[128,2,1024]{2,1,0:T(2,128)(2,1)} %bitcast.11, ...), custom_call_target="tpu_custom_call" | custom-call | tf_op jit(solution)/shard_map/pallas_call | solution.py:249
  27.2 1.5 %copy.11 = bf16[1,1,4,8192]{3,2,1,0:T(4,128)(2,1)} copy(bf16[1,1,4,8192]{3,2,1,0:T(4,128)(2,1)} %bitcast.13) | data formatting | bytes 131072

commit v8 on v7

--- a/solution.py
+++ b/solution.py
@@ -13,7 +13,7 @@
 NEG = -1e30
 SCALE = math.log2(math.e) * HEAD_SIZE ** (-0.5)
 FLOOR = -1e29
-PAIR = 2
+PAIR = 1
 FEW = 4
 MESH = pl.DeviceIdType.MESH
 F32 = jnp.float32

time: 28.8 us -> 29.8 us (1.035)
  Pallas kernels: 26.5 us -> 27.5 us
    pallas_call x1, Pallas kernels: 26.5 us -> 27.5 us  [per_device(): pl.pallas_call(functools.partial(kernel, samples, prompts), out_shape=jax...]
where the time goes in v8:
time: 29.8 us; the launch traced here: 29.6 us
  Pallas kernels  27.5 us (92%)
  local copies, waits for them, and re-layouts  1.49 us (5%)
  between operations  0.66 us (2%)
    pallas_call x1, Pallas kernels, per_device(): pl.pallas_call(functools.partial(kernel, samples, prompts), out_shape=jax...  27.5 us
    unnamed x1, local copies, waits for them, and re-layouts  1.49 us

profile of v8, /device:TPU:0, one launch (start us, length us, event | category | flops | bytes accessed | tf_op | source)
XLA Modules:
  0.0 29.6 jit_solution(7281264405296502214)
XLA Ops:
  0.7 27.5 %shard_map.73 = bf16[8,32,128]{2,1,0:T(8,128)(2,1)} custom-call(s32[8]{0:T(128)} %plen_hbm.1, s32[1,1]{1,0:T(1,128)S(6)} %copy.10.slen_hbm, bf16[4,8192]{1,0:T(4,128)(2,1)} %bitcast.14, bf16[4,2,1024]{2,1,0:T(2,128)(2,1)} %bitcast.15, bf16[256,2,1024]{2,1,0:T(2,128)(2,1)} %bitcast.10, bf16[128,2,1024]{2,1,0:T(2,128)(2,1)} %bitcast.11, ...), custom_call_target="tpu_custom_call" | custom-call | tf_op jit(solution)/shard_map/pallas_call | solution.py:249
  28.1 1.5 %copy.11 = bf16[1,1,4,8192]{3,2,1,0:T(4,128)(2,1)} copy(bf16[1,1,4,8192]{3,2,1,0:T(4,128)(2,1)} %bitcast.13) | data formatting | bytes 131072
